TPU v7x, 128 devices: a whole 4x4x4 slice. The times are simulated.
128 devices in a mesh: ctx: 32 (over x_lo, z, y), tp: 4 (over x_hi, core).
Axes of the slice: x: 4 (x_hi: 2, x_lo: 2; x = x_hi * 2 + x_lo), y: 4, z: 4, core: 2. Of those that a mesh axis runs over, the one named last changes fastest.
Arguments:
- stream_one: bfloat16 [12288, 8192], P('ctx', 'tp'), may hold values from -6 to 6
- stream_two: bfloat16 [12288, 8192], P('ctx', 'tp'), may hold values from -6 to 6
- stream_value: bfloat16 [12288, 8192], P('ctx', 'tp'), may hold values from -6 to 6
- short_stream_taps: bfloat16 [3, 7, 8192], P(None, None, 'tp'), may hold values from -6 to 6
- medium_filter: bfloat16 [512, 128], P('tp'), may hold values from -1.25 to 1.25
- residual: bfloat16 [12288, 8192], P('ctx', 'tp'), may hold values from -60 to 60
- norm_gain: bfloat16 [8192], P('tp'), may hold values from 0.5 to 1.5
- queries: bfloat16 [12288, 4096], P('ctx', 'tp'), may hold values from -12 to 12
- keys: bfloat16 [12288, 512], P('ctx', 'tp'), may hold values from -6 to 6
- values: bfloat16 [12288, 512], P('ctx', 'tp'), may hold values from -6 to 6
Outputs:
- normed: bfloat16 [12288, 8192], P('ctx', 'tp')
- attended: bfloat16 [12288, 4096], P('ctx', 'tp')
All inputs are finite; a program needn't handle non-finite values.
Results may differ from a plain program's by a relative error of at most 0.0065.
Values may be sent and summed in bfloat16 or wider, within the bound.
No kernel may reach another device: no remote copies, remote signals or barrier semaphores. Data moves between devices by JAX's collectives and lax.ppermute only.
A program may use at most 128 MiB of HBM per device.

v0:
```python
import functools
import math

import jax
import jax.numpy as jnp
import numpy as np
from jax import lax
from jax.experimental import pallas as pl
from jax.experimental.pallas import tpu as pltpu
from jax.sharding import PartitionSpec as P

f32=jnp.float32; bf=jnp.bfloat16
SHORT=7; GROUP=16; LANES=128; EDGE=16; TAPS=128; BLK=64
LIGHT = pl.CostEstimate(flops=1000, bytes_accessed=1000, transcendentals=0)

def tail_kernel(one, two, val, taps, out, x_scr):
    keep = TAPS
    last = one.shape[0]
    for lanes in range(one.shape[1] // LANES):
        c = slice(lanes * LANES, (lanes + 1) * LANES)
        t = taps[:, :, c].astype(f32)

        def short(ref, which, slot):
            x_scr[slot] = ref[last - keep - EDGE:, c].astype(f32)
            total = t[which, 0:1] * x_scr[slot, EDGE:EDGE + keep, :]
            for j in range(1, SHORT):
                total += t[which, j:j + 1] * x_scr[slot, EDGE - j:EDGE - j + keep, :]
            return total
        out[0:keep, c] = (short(one, 0, 2 * (lanes % 2)) * short(val, 2, 2 * (lanes % 2) + 1)).astype(bf)
    for n, ref in enumerate((one, two, val)):
        out[keep + EDGE * n:keep + EDGE * (n + 1)] = ref[last - EDGE:, :]


def tail_call(one, two, val, taps):
    rows, width = one.shape
    tile = 4 * LANES
    spec = pl.BlockSpec((rows // 2, tile), lambda i: (1, i))
    out_rows = TAPS + 3 * EDGE
    return pl.pallas_call(tail_kernel, grid=(width // tile,),
        in_specs=[spec] * 3 + [pl.BlockSpec((3, SHORT, tile), lambda i: (0, 0, i))],
        out_specs=pl.BlockSpec((out_rows, tile), lambda i: (0, i)),
        out_shape=jax.ShapeDtypeStruct((out_rows, width), bf),
        scratch_shapes=[pltpu.VMEM((4, TAPS + EDGE, LANES), f32)],
        cost_estimate=LIGHT,
        name="mixed_tail")(one, two, val, taps)


def mixer_kernel(one, two, val, halo, taps, rev, res, branch, squares, x_scr, m_scr, t_scr):
    rows = one.shape[0]
    t = taps[...].astype(f32)
    def short(ref, n):
        lo = TAPS + EDGE * n
        x_scr[n, 0:EDGE] = halo[lo:lo + EDGE, :].astype(f32)
        x_scr[n, EDGE:] = ref[...].astype(f32)
        total = t[n, 0:1] * x_scr[n, EDGE:, :]
        for j in range(1, SHORT):
            total += t[n, j:j + 1] * x_scr[n, EDGE - j:EDGE - j + rows, :]
        return total
    m_scr[0:TAPS] = halo[0:TAPS]
    m_scr[TAPS:] = (short(one, 0) * short(val, 2)).astype(bf)
    gate = short(two, 1)
    groups = LANES // GROUP
    for g in range(groups):
        row = jnp.broadcast_to(rev[g:g + 1, :], (BLK, 2 * TAPS))
        rolled = pltpu.roll(row, 0, 1, stride=1, stride_axis=0)
        t_scr[g * BLK:(g + 1) * BLK] = rolled.astype(bf)
    lane = lax.broadcasted_iota(jnp.int32, (BLK, LANES), 1) // GROUP
    span = BLK + TAPS
    total = jnp.zeros((8, 128), f32)
    for pair in range(rows // (2 * BLK)):
        at = 2 * BLK * pair
        window = jnp.concatenate([m_scr[at:at + span], m_scr[at + BLK:at + BLK + span]], axis=1)
        wide = jnp.dot(t_scr[:, :span], window, preferred_element_type=f32)
        for half in range(2):
            r = slice(at + BLK * half, at + BLK * (half + 1))
            c = slice(LANES * half, LANES * (half + 1))
            medium = wide[0:BLK, c]
            for g in range(1, groups):
                medium = jnp.where(lane == g, wide[g * BLK:(g + 1) * BLK, c], medium)
            summed = res[r].astype(f32) + gate[r] * medium
            branch[r] = summed
            sq = summed * summed
            @pl.when(pl.program_id(0) == 0)
            def _(): squares[r] = sq
            @pl.when(pl.program_id(0) > 0)
            def _(): squares[r] += sq

def mixer_call(one, two, val, halo, taps, rev, res):
    rows, width = one.shape
    spec = pl.BlockSpec((rows, LANES), lambda i: (0, i))
    groups = LANES // GROUP
    return pl.pallas_call(mixer_kernel, grid=(width // LANES,),
        in_specs=[spec] * 3 + [pl.BlockSpec((halo.shape[0], LANES), lambda i: (0, i)),
            pl.BlockSpec((3, SHORT, LANES), lambda i: (0, 0, i)),
            pl.BlockSpec((groups, 2 * TAPS), lambda i: (i, 0)), spec],
        out_specs=[spec, pl.BlockSpec((rows, LANES), lambda i: (0, 0))],
        out_shape=[jax.ShapeDtypeStruct((rows, width), f32), jax.ShapeDtypeStruct((rows, LANES), f32)],
        scratch_shapes=[pltpu.VMEM((3, EDGE + rows, LANES), f32), pltpu.VMEM((TAPS + rows, LANES), bf),
            pltpu.VMEM((groups * BLK, 2 * TAPS), bf)],
        compiler_params=pltpu.CompilerParams(vmem_limit_bytes=32 * 2**20),
        cost_estimate=LIGHT,
        name="mixer")(one, two, val, halo, taps, rev, res)

def reversed_taps(filters):
    flipped = filters.astype(f32)[:, ::-1]
    return jnp.pad(flipped, ((0, 0), (1, TAPS - 1)))


HD = 128
QUAD = 4
ONES = 16
EMPTY, FULL, DIAGONAL = 0, 1, 2
DUMMIES = 3
SCALE = math.log2(math.e) / math.sqrt(HD)


def pack_kernel(keys, values, queries, packed, given, sem):
    middle = given.shape[1]
    copy = pltpu.make_async_copy(queries.at[:, middle:], given, sem)
    copy.start()
    packed[:, :HD] = keys[...]
    turned = values[...].astype(f32).T.astype(bf)
    for part in range(values.shape[0] // HD):
        packed[part * HD:(part + 1) * HD, HD:] = turned[:, part * HD:(part + 1) * HD]
    copy.wait()


def pack_call(keys, values, queries):
    hbm = pl.BlockSpec(memory_space=pltpu.HBM)
    vmem = pl.BlockSpec(memory_space=pltpu.VMEM)
    return pl.pallas_call(pack_kernel, in_specs=[vmem, vmem, hbm], out_specs=[vmem, hbm],
                          out_shape=[jax.ShapeDtypeStruct((keys.shape[0], 2 * HD), bf),
                                     jax.ShapeDtypeStruct((queries.shape[0], queries.shape[1] // 2), bf)],
                          scratch_shapes=[pltpu.SemaphoreType.DMA], name="pack_keys")(keys, values, queries)


def turn_kernel(queries, turned):
    rows = queries.shape[0]
    for head in range(QUAD):
        wide = queries[:, head * HD:(head + 1) * HD].astype(f32).T * SCALE
        high = wide.astype(bf)
        columns = slice(head * rows, (head + 1) * rows)
        turned[0, :HD, columns] = high
        turned[0, HD:, columns] = (wide - high.astype(f32)).astype(bf)


def turn_call(queries):
    rows, width = queries.shape
    quads = width // (QUAD * HD)
    return pl.pallas_call(turn_kernel, grid=(quads,),
        in_specs=[pl.BlockSpec((rows, QUAD * HD), lambda i: (0, i))],
        out_specs=pl.BlockSpec((1, 2 * HD, QUAD * rows), lambda i: (i, 0, 0)),
        out_shape=jax.ShapeDtypeStruct((quads, 2 * HD, QUAD * rows), bf),
        cost_estimate=LIGHT,
        name="turn_queries")(queries)


def table_layout(shards):
    slots = shards + DUMMIES + (shards + DUMMIES) % 2
    at_a = 2 + DUMMIES
    at_b = at_a + shards
    at_live = at_b + shards
    at_fast = at_live + slots
    at_slow = at_fast + 3 * (slots // 2)
    return slots, at_a, at_b, at_live, at_fast, at_slow, at_slow + 3 * (slots // 2)


def attend_kernel(sizes, groups, starts, last, rows, *refs):
    refs = list(refs)
    take = lambda n: [refs.pop(0) for _ in range(n)]
    table, = take(1)
    pieces = take(len(sizes))
    q_in = take(len(groups))
    state_in = [None if start else take(2) for start in starts]
    results = take(len(groups)) if last else [take(2) for _ in groups]
    q, kv, acc, top, s_scr, p_scr, a_scr, load_sem, kv_sem, store_sem = refs
    shards = sum(sizes)
    slots, at_a, at_b, at_live, at_fast, at_slow, _ = table_layout(shards)
    me = lax.axis_index("ctx")
    n_fast = table[me, 0]
    n_slow = table[me, 1]
    half = 2 * rows
    parts = rows // HD

    copies = []
    number = 0
    for piece, size in zip(pieces, sizes):
        for index in range(size):
            for n, at in enumerate((at_a, at_b)):
                slot = table[me, at + number]
                copies.append((slot, pltpu.make_async_copy(
                    piece.at[index], kv.at[jnp.maximum(slot, 0)], kv_sem.at[2 * number + n])))
            number += 1
    for slot, copy in copies:
        pl.when(slot >= 0)(copy.start)
    loads = []
    at = 0
    for n, count in enumerate(groups):
        group = pl.ds(at, count)
        loads.append(pltpu.make_async_copy(q_in[n], q.at[group], load_sem.at[3 * n]))
        if not starts[n]:
            loads.append(pltpu.make_async_copy(state_in[n][0], acc.at[group], load_sem.at[3 * n + 1]))
            loads.append(pltpu.make_async_copy(state_in[n][1], top.at[group], load_sem.at[3 * n + 2]))
        at += count
    for copy in loads:
        copy.start()
    at = 0
    for n, count in enumerate(groups):
        if starts[n]:
            for quad in range(at, at + count):
                acc[quad] = jnp.zeros(acc.shape[1:], f32)
                top[quad] = jnp.full(top.shape[1:], -1e30, f32)
        at += count
    for slot, copy in copies:
        pl.when(slot >= 0)(copy.wait)
    for copy in loads:
        copy.wait()
    for n in range(DUMMIES):
        slot = table[me, 2 + n]

        @pl.when(slot >= 0)
        def _():
            kv[slot, :, HD:] = jnp.zeros((rows, HD), bf)

    def decode(code):
        return code % 4, (code // 4) % 64, (code // 256) % 4, (code // 1024) % 4

    def columns(pair):
        return slice(pair * half, (pair + 1) * half)

    def multiply_keys(quad, block, pair):
        k = jnp.concatenate([kv[2 * block, :, :HD], kv[2 * block + 1, :, :HD]], axis=0)
        k = jnp.concatenate([k, k], axis=1)
        return jnp.dot(k, q[quad, :, columns(pair)], preferred_element_type=f32)

    def multiply_values(quad, block, pair, weights, factor):
        v = jnp.concatenate([kv[2 * block + n // parts, (n % parts) * HD:(n % parts + 1) * HD, HD:]
                             for n in range(2 * parts)], axis=1)
        live = [jnp.full((ONES, rows), table[me, at_live + 2 * block + n].astype(f32)).astype(bf) for n in range(2)]
        v = jnp.concatenate([v, jnp.concatenate(live, axis=1)], axis=0)
        c = columns(pair)
        acc[quad, :, c] = acc[quad, :, c] * factor + jnp.dot(v, weights, preferred_element_type=f32)

    def soften(quad, pair, s):
        c = columns(pair)
        old = top[quad, 0:1, c]
        new = jnp.maximum(old, jnp.max(s, axis=0, keepdims=True))
        top[quad, 0:1, c] = new
        return jnp.exp2(s - new).astype(bf), jnp.exp2(old - new)

    @pl.loop(0, n_slow)
    def _(number):
        quad, block, *modes = decode(table[me, at_slow + number])
        for pair in range(2):
            s_scr[...] = multiply_keys(quad, block, pair)
            key = lax.broadcasted_iota(jnp.int32, (rows, rows), 0)
            query = lax.broadcasted_iota(jnp.int32, (rows, rows), 1)
            for part, mode in enumerate(modes):
                limit = jnp.where(mode == FULL, rows, jnp.where(mode == DIAGONAL, 0, -2 * rows))
                allowed = key - query <= limit
                for head in range(2):
                    r = slice(part * rows, (part + 1) * rows)
                    c = slice(head * rows, (head + 1) * rows)
                    s_scr[r, c] = jnp.where(allowed, s_scr[r, c], -1e30)
            weights, factor = soften(quad, pair, s_scr[...])
            multiply_values(quad, block, pair, weights, factor)

    def fast_entry(number):
        return decode(table[me, at_fast + jnp.clip(number, 0, n_fast - 1)])[:2]

    def region(number, unroll):
        todo = [(*fast_entry(number + n), pair) for n in range(unroll) for pair in range(2)]
        todo.append((*fast_entry(number + unroll), 0))
        s = s_scr[...]
        pending = (*fast_entry(number - 1), 1, p_scr[...], a_scr[0:1])
        for now, later in zip(todo, todo[1:]):
            coming = multiply_keys(*later)
            multiply_values(*pending)
            quad, block, pair = now
            weights, factor = soften(quad, pair, s)
            pending = (quad, block, pair, weights, factor)
            s = coming
        s_scr[...] = s
        p_scr[...] = pending[3]
        a_scr[0:1] = pending[4]

    @pl.when(n_fast > 0)
    def _():
        s_scr[...] = multiply_keys(*fast_entry(0), 0)
        p_scr[...] = jnp.zeros_like(p_scr)
        a_scr[...] = jnp.ones_like(a_scr)

        @pl.loop(0, n_fast // 2)
        def _(step):
            region(2 * step, 2)

        @pl.when(n_fast % 2 == 1)
        def _():
            region(n_fast - 1, 1)

        multiply_values(*fast_entry(n_fast - 1), 1, p_scr[...], a_scr[0:1])

    if last:
        at = 0
        for n, count in enumerate(groups):
            for quad in range(count):
                for head in range(QUAD):
                    c = slice(head * rows, (head + 1) * rows)
                    value = acc[at + quad, :HD, c] / acc[at + quad, HD:HD + 1, c]
                    to = (quad * QUAD + head) * HD
                    results[n][:, to:to + HD] = value.T.astype(bf)
            at += count
    else:
        stores = []
        at = 0
        for n, count in enumerate(groups):
            group = pl.ds(at, count)
            stores.append(pltpu.make_async_copy(acc.at[group], results[n][0], store_sem.at[2 * n]))
            stores.append(pltpu.make_async_copy(top.at[group], results[n][1], store_sem.at[2 * n + 1]))
            at += count
        for copy in stores:
            copy.start()
        for copy in stores:
            copy.wait()


def attend_call(table, pieces, turned, states, last=False):
    wide = turned[0].shape[2]
    rows = wide // QUAD
    sizes = tuple(piece.shape[0] for piece in pieces)
    shards = sum(sizes)
    slots = table_layout(shards)[0]
    groups = tuple(t.shape[0] for t in turned)
    quads = sum(groups)
    starts = tuple(state is None for state in states)
    hbm = pl.BlockSpec(memory_space=pltpu.HBM)
    operands = [table, *pieces, *turned] + [part for state in states if state is not None for part in state]
    if last:
        out_shape = [jax.ShapeDtypeStruct((rows, count * QUAD * HD), bf) for count in groups]
        out_specs = [pl.BlockSpec(memory_space=pltpu.VMEM)] * len(groups)
    else:
        out_shape = []
        for count in groups:
            out_shape.append(jax.ShapeDtypeStruct((count, HD + ONES, wide), f32))
            out_shape.append(jax.ShapeDtypeStruct((count, 8, wide), f32))
        out_specs = [hbm] * len(out_shape)
    result = pl.pallas_call(
        functools.partial(attend_kernel, sizes, groups, starts, last, rows),
        in_specs=[pl.BlockSpec(memory_space=pltpu.SMEM)] + [hbm] * (len(operands) - 1),
        out_specs=out_specs,
        out_shape=out_shape,
        scratch_shapes=[
            pltpu.VMEM((quads, 2 * HD, wide), bf),
            pltpu.VMEM((slots, rows, 2 * HD), bf),
            pltpu.VMEM((quads, HD + ONES, wide), f32),
            pltpu.VMEM((quads, 8, wide), f32),
            pltpu.VMEM((2 * rows, 2 * rows), f32),
            pltpu.VMEM((2 * rows, 2 * rows), bf),
            pltpu.VMEM((8, 2 * rows), f32),
            pltpu.SemaphoreType.DMA((3 * len(groups),)),
            pltpu.SemaphoreType.DMA((2 * shards,)),
            pltpu.SemaphoreType.DMA((2 * len(groups),)),
        ],
        compiler_params=pltpu.CompilerParams(vmem_limit_bytes=48 * 2**20),
        cost_estimate=LIGHT,
        name="attend",
    )(*operands)
    if last:
        return list(result)
    return [tuple(result[2 * n:2 * n + 2]) for n in range(len(groups))]


def make_table(sources_of, wants_of):
    lines = []
    for me, sources in enumerate(sources_of):
        shards = len(sources)
        slots, at_a, at_b, at_live, at_fast, at_slow, size = table_layout(shards)
        line = np.zeros(size, np.int32)
        line[2:at_live] = -1
        line[at_live:at_fast] = 1
        fast, slow, dummies = [], [], []
        used = 0

        def place(members):
            nonlocal used
            modes = []
            for shard, mode in members:
                line[at_a + shard] = used
                used += 1
                modes.append(mode)
            if len(members) % 2:
                line[at_b + members[-1][0]] = used
                line[at_live + used] = 0
                dummies.append(used)
                used += 1
                modes.append(FULL if members[-1][1] == FULL else EMPTY)
            return [((used - len(modes)) // 2 + n, modes[2 * n], modes[2 * n + 1]) for n in range(len(modes) // 2)]

        shared = []
        placed = set()
        for quads, position, skipped in wants_of[me]:
            new = [(n, FULL if source < position else DIAGONAL) for n, source in enumerate(sources)
                   if source <= position and source not in skipped and n not in placed]
            new.sort(key=lambda member: member[1])
            blocks = place(new)
            placed.update(n for n, _ in new)
            for quad in quads:
                for block, one, two in shared + blocks:
                    code = quad + 4 * block
                    if (one, two) == (FULL, FULL):
                        fast.append(code)
                    else:
                        slow.append(code + 256 * one + 1024 * two)
            shared = shared + [(block, FULL, FULL) for block, _, _ in blocks]
        assert used <= slots and len(dummies) <= DUMMIES
        line[0], line[1] = len(fast), len(slow)
        line[2:2 + len(dummies)] = dummies
        line[at_fast:at_fast + len(fast)] = fast
        line[at_slow:at_slow + len(slow)] = slow
        lines.append(line)
    return np.array(lines)


D = 8192
Z = Y = 4
PLANE = Z * Y
BLOCKS = 2 * PLANE
SHARED = 9


def neighbour(i, x=0, z=0, y=0):
    at_x, at_z, at_y = i // PLANE, (i // Y) % Z, i % Y
    return (at_x + x) % 2 * PLANE + (at_z + z) % Z * Y + (at_y + y) % Y


def mirrored(i):
    return BLOCKS - 1 - i


def moved(value, x=0, z=0, y=0):
    return lax.ppermute(value, "ctx", [(i, neighbour(i, x, z, y)) for i in range(BLOCKS)])


def near_line(first, last, axis):
    return [first, moved(first, **{axis: 1}), moved(first, **{axis: -1}), moved(last, **{axis: 2})]


def sources_of(me, plane, axis, other):
    base = neighbour(me, x=plane)
    line = [neighbour(base, **{axis: -step}) for step in (0, 1, -1, 2)]
    lines = [[neighbour(b, **{other: -step}) for b in line] for step in (1, -1, 2)]
    return [base] + line[1:], lines[0] + lines[1], lines[2]


def wants(me):
    found = [((0,) if mirrored(me) < SHARED else (0, 1), me, ())]
    if me < SHARED:
        found.append(((2,), mirrored(me), ()))
    return found


def tables():
    everyone = range(BLOCKS)
    stages = [[sources_of(me, 0, "z", "y")[n] + sources_of(me, 1, "y", "z")[n] for me in everyone] for n in range(3)]
    return [make_table(stage, [wants(me) for me in everyone]) for stage in stages]


def shards(stream_one, stream_two, stream_value, short_stream_taps, medium_filter, residual, norm_gain, queries, keys, values):
    rows, width = stream_one.shape
    middle = queries.shape[1] // 2
    me = lax.axis_index("ctx")
    own, given = pack_call(keys, values, queries)
    other = moved(own, x=1)
    given = lax.ppermute(given, "ctx", [(mirrored(i), i) for i in range(SHARED)])
    same, other = lax.optimization_barrier((own, other))
    a = near_line(same, same, "z")
    b = near_line(other, other, "y")
    a, b = lax.optimization_barrier((a, b))
    a_line, b_line = jnp.stack(a), jnp.stack(b)
    lines = [moved(a_line, y=1), moved(a_line, y=-1), moved(b_line, z=1), moved(b_line, z=-1)]
    tail = tail_call(stream_one, stream_two, stream_value, short_stream_taps)
    halo = lax.ppermute(tail, "ctx", [(i, i + 1) for i in range(BLOCKS - 1)])
    near, far, across = tables()
    turned = [turn_call(queries), turn_call(given)]
    states = attend_call(near, [part[None] for part in a + b], turned, [None, None])
    a_line, b_line, states = lax.optimization_barrier((a_line, b_line, states))
    crossed = [moved(a_line, y=2), moved(b_line, z=2)]
    states = attend_call(far, lines, turned, states)
    kept, helped = attend_call(across, crossed, turned, states, last=True)
    returned = lax.ppermute(helped, "ctx", [(i, mirrored(i)) for i in range(SHARED)])
    halo, helped = lax.optimization_barrier((halo, helped))
    branch, squares = mixer_call(stream_one, stream_two, stream_value, halo, short_stream_taps, reversed_taps(medium_filter), residual)
    sums = jnp.sum(squares, axis=1)
    sums, returned = lax.optimization_barrier((sums, returned))
    parts = [lax.ppermute(sums, "tp", [(i, i ^ step) for i in range(4)]) for step in (1, 2, 3)]
    later = jnp.where(me > BLOCKS - 1 - SHARED, returned, kept[:, middle:])
    attended = jnp.concatenate([kept[:, :middle], later], axis=1)
    scaling = lax.rsqrt((sums + parts[0] + parts[1] + parts[2]) / D + 1e-06)
    normed = (branch * scaling[:, None] * norm_gain.astype(f32)[None, :]).astype(bf)
    return normed, attended


def solution(mesh):
    in_specs = (P("ctx", "tp"), P("ctx", "tp"), P("ctx", "tp"), P(None, None, "tp"), P("tp", None),
                P("ctx", "tp"), P("tp"), P("ctx", "tp"), P("ctx", "tp"), P("ctx", "tp"))
    return jax.shard_map(shards, mesh=mesh, in_specs=in_specs, out_specs=(P("ctx", "tp"), P("ctx", "tp")), check_vma=False)
```

profile of v0, /device:TPU:17, one launch (start us, length us, event | category | flops | bytes accessed | tf_op | source)
XLA Modules:
  0.0 174.0 jit_solution(5328311323192996446)
XLA Ops:
  0.6 14.6 %pack_keys.1 = (bf16[384,256]{1,0:T(8,128)(2,1)}, bf16[384,512]{1,0:T(8,128)(2,1)}) custom-call(bf16[384,128]{1,0:T(8,128)(2,1)} %keys.1, bf16[384,128]{1,0:T(8,128)(2,1)} %values.1, bf16[384,1024]{1,0:T(8,128)(2,1)} %queries.3), custom_call_target="tpu_custom_call" | custom-call | tf_op jit(solution)/shard_map/pack_keys/pallas_call | solution.py:131
  15.3 0.0 copy-start.30
  15.3 1.3 collective-permute-start.1
  16.6 4.8 %collective-permute-done.1 = bf16[384,256]{1,0:T(8,128)(2,1)S(1)} collective-permute-done((bf16[384,256]{1,0:T(8,128)(2,1)}, bf16[384,256]{1,0:T(8,128)(2,1)S(1)}, u32[]{:S(2)}, u32[]{:S(2)}) %collective-permute-start.1) | collective-permute-done | bytes 196640 | tf_op jit(solution)/shard_map/ppermute | solution.py:441
  21.3 1.6 collective-permute-start.2
  23.0 2.1 %collective-permute-start.3 = (bf16[384,256]{1,0:T(8,128)(2,1)}, bf16[384,256]{1,0:T(8,128)(2,1)S(1)}, u32[]{:S(2)}, u32[]{:S(2)}) collective-permute-start(bf16[384,256]{1,0:T(8,128)(2,1)} %get-tuple-element.38), channel_id=1, source_target_pairs={{0,48},{4,52},{8,56},{12,60},{16,0},{20,4},{24,8},{28,12},{32,16},... | collective-permute-start | bytes 589832 | tf_op jit(solution)/shard_map/ppermute | solution.py:441
  25.1 1.3 collective-permute-start.4
  26.4 1.0 collective-permute-start.5
  27.4 0.5 collective-permute-start.6
  27.9 1.1 collective-permute-done.2
  29.0 0.2 collective-permute-start.7
  29.2 0.0 collective-permute-done.3
  29.2 4.9 %collective-permute-done.4 = bf16[384,256]{1,0:T(8,128)(2,1)S(1)} collective-permute-done((bf16[384,256]{1,0:T(8,128)(2,1)}, bf16[384,256]{1,0:T(8,128)(2,1)S(1)}, u32[]{:S(2)}, u32[]{:S(2)}) %collective-permute-start.4) | collective-permute-done | bytes 196640 | tf_op jit(solution)/shard_map/ppermute | solution.py:441
  34.1 2.0 %collective-permute-done.7 = bf16[384,256]{1,0:T(8,128)(2,1)S(1)} collective-permute-done((bf16[384,256]{1,0:T(8,128)(2,1)S(1)}, bf16[384,256]{1,0:T(8,128)(2,1)S(1)}, u32[]{:S(2)}, u32[]{:S(2)}) %collective-permute-start.7) | collective-permute-done | bytes 196640 | tf_op jit(solution)/shard_map/ppermute | solution.py:441
  36.1 1.0 pad_maximum_fusion.1
  37.1 0.7 copy-done.15
  37.8 0.7 collective-permute-start.13
  38.5 1.3 collective-permute-start.8
  39.7 1.4 collective-permute-start.14
  41.2 2.4 %turn_queries.2.refs_9_.refs_5_.refs_3_ = bf16[2,256,1536]{2,1,0:T(8,128)(2,1)} custom-call(bf16[384,1024]{1,0:T(8,128)(2,1)} %queries.3), custom_call_target="tpu_custom_call" | custom-call | flops 1000 | bytes 1000 | tf_op jit(solution)/shard_map/turn_queries/pallas_call | solution.py:150
  43.6 1.0 pad_maximum_fusion
  44.5 2.0 %collective-permute-start.11 = (bf16[4,384,256]{2,1,0:T(8,128)(2,1)}, bf16[4,384,256]{2,1,0:T(8,128)(2,1)}, u32[]{:S(2)}, u32[]{:S(2)}) collective-permute-start(bf16[4,384,256]{2,1,0:T(8,128)(2,1)} %pad_maximum_fusion), channel_id=1, source_target_pairs={{0,4},{4,8},{8,12},{12,0},{16,20},{20,24},{24,28},{28,16},{32,36},... | collective-permute-start | bytes 2359304 | tf_op jit(solution)/shard_map/ppermute | solution.py:441
  46.5 0.0 collective-permute-start.12
  46.5 3.6 %collective-permute-done.8.queries = bf16[384,512]{1,0:T(8,128)(2,1)S(1)} collective-permute-done((bf16[384,512]{1,0:T(8,128)(2,1)S(1)}, bf16[384,512]{1,0:T(8,128)(2,1)S(1)}, u32[]{:S(2)}, u32[]{:S(2)}) %collective-permute-start.8) | collective-permute-done | bytes 393248 | tf_op jit(solution)/shard_map/ppermute | solution.py:474
  50.2 0.8 copy-done.27
  50.9 2.1 %turn_queries.3.refs_10_.refs_6_.refs_4_ = bf16[1,256,1536]{2,1,0:T(8,128)(2,1)} custom-call(bf16[384,512]{1,0:T(8,128)(2,1)} %copy-done.27), custom_call_target="tpu_custom_call" | custom-call | flops 1000 | bytes 1000 | tf_op jit(solution)/shard_map/turn_queries/pallas_call | solution.py:150
  53.0 1.1 copy-done.2
  54.2 0.9 copy-done.16
  55.1 0.9 copy-done.18
  56.0 0.9 copy-done.20
  57.0 18.9 %attend.3 = (f32[2,144,1536]{2,1,0:T(8,128)}, f32[2,8,1536]{2,1,0:T(8,128)S(1)}, f32[1,144,1536]{2,1,0:T(8,128)S(1)}, f32[1,8,1536]{2,1,0:T(8,128)S(1)}) custom-call(s32[32,69]{1,0:T(8,128)S(1)} %copy-done.26, bf16[1,384,256]{2,1,0:T(8,128)(2,1)S(1)} %bitcast.9, bf16[1,384,256]{2,1,0:T(8,128)(2,1)S(1)} %bitcast.13, bf16[1,384,256]{2,1,0:T(8,128)(2,1)S(1)} %bitcast.15, ...), custom_call_target="tpu_custom_call" | custom-call | flops 1000 | bytes 1000 | tf_op jit(solution)/shard_map/attend/pallas_call | solution.py:347
  75.9 0.6 copy-done.22
  76.5 0.0 collective-permute-start.10
  76.5 2.0 %collective-permute-start.9 = (bf16[4,384,256]{2,1,0:T(8,128)(2,1)}, bf16[4,384,256]{2,1,0:T(8,128)(2,1)S(1)}, u32[]{:S(2)}, u32[]{:S(2)}) collective-permute-start(bf16[4,384,256]{2,1,0:T(8,128)(2,1)} %pad_maximum_fusion), channel_id=1, source_target_pairs={{0,8},{4,12},{8,0},{12,4},{16,24},{20,28},{24,16},{28,20},{32,40},... | collective-permute-start | bytes 2359304 | tf_op jit(solution)/shard_map/ppermute | solution.py:441
  78.5 4.3 %mixed_tail.1 = bf16[176,2048]{1,0:T(8,128)(2,1)} custom-call(bf16[384,2048]{1,0:T(8,128)(2,1)} %one.3, bf16[384,2048]{1,0:T(8,128)(2,1)} %two.3, bf16[384,2048]{1,0:T(8,128)(2,1)} %val.3, bf16[3,7,2048]{2,1,0:T(8,128)(2,1)} %taps.3), custom_call_target="tpu_custom_call" | custom-call | flops 1000 | bytes 1000 | tf_op jit(solution)/shard_map/mixed_tail/pallas_call | solution.py:39
  82.8 0.0 collective-permute-done.14.refs_4_
  82.8 2.8 %collective-permute-start = (bf16[176,2048]{1,0:T(8,128)(2,1)}, bf16[176,2048]{1,0:T(8,128)(2,1)}, u32[]{:S(2)}, u32[]{:S(2)}) collective-permute-start(bf16[176,2048]{1,0:T(8,128)(2,1)} %mixed_tail.1), channel_id=1, source_target_pairs={{0,4},{4,8},{8,12},{12,16},{16,20},{20,24},{24,28},{28,32},{32,36}... | collective-permute-start | bytes 2162696 | tf_op jit(solution)/shard_map/ppermute | solution.py:482
  85.7 0.0 collective-permute-done.12.refs_2_
  85.7 22.4 %attend.4 = (f32[2,144,1536]{2,1,0:T(8,128)}, f32[2,8,1536]{2,1,0:T(8,128)S(1)}, f32[1,144,1536]{2,1,0:T(8,128)S(1)}, f32[1,8,1536]{2,1,0:T(8,128)S(1)}) custom-call(s32[32,117]{1,0:T(8,128)S(1)} %copy-done.25, bf16[4,384,256]{2,1,0:T(8,128)(2,1)} %collective-permute-done.11.refs_1_, bf16[4,384,256]{2,1,0:T(8,128)(2,1)} %collective-permute-done.12.refs_2_, ...), custom_call_target="tpu_custom_call" | custom-call | flops 1000 | bytes 1000 | tf_op jit(solution)/shard_map/attend/pallas_call | solution.py:347
  108.1 0.0 collective-permute-done.10.refs_2_
  108.1 0.0 collective-permute-done.9.refs_1_
  108.1 0.0 copy-start.10
  108.1 0.9 copy-done.10
  109.0 1.1 copy-done.11
  110.1 18.8 %attend.5 = (bf16[384,1024]{1,0:T(8,128)(2,1)S(1)}, bf16[384,512]{1,0:T(8,128)(2,1)}) custom-call(s32[32,69]{1,0:T(8,128)S(1)} %copy-done.24, bf16[4,384,256]{2,1,0:T(8,128)(2,1)S(1)} %copy-done.11, bf16[4,384,256]{2,1,0:T(8,128)(2,1)S(1)} %collective-permute-done.10.refs_2_, bf16[2,256,1536]{2,1,0:T(8,128)(2,1)S(1)} %copy-done.1, ...), custom_call_target="tpu_custom_call" | custom-call | flops 1000 | bytes 1000 | tf_op jit(solution)/shard_map/attend/pallas_call | solution.py:347
  128.9 0.0 copy-start.12
  128.9 0.9 copy-done.12
  129.8 1.3 collective-permute-start.15
  131.1 0.1 rev.3
  131.2 0.1 pad.4.rev
  131.4 0.0 copy-start.5
  131.4 1.4 copy-done.5
  132.8 1.4 copy-done.6
  134.2 1.4 copy-done.9
  135.6 21.9 %mixer.1 = (f32[384,2048]{1,0:T(8,128)S(1)}, f32[384,128]{1,0:T(8,128)S(1)}) custom-call(bf16[384,2048]{1,0:T(8,128)(2,1)S(1)} %copy-done.4, bf16[384,2048]{1,0:T(8,128)(2,1)S(1)} %copy-done.5, bf16[384,2048]{1,0:T(8,128)(2,1)S(1)} %copy-done.6, bf16[176,2048]{1,0:T(8,128)(2,1)} %collective-permute-done.halo, bf16[3,7,2048]{2,1,0:T(8,128)(2,1)S(1)} %copy-done.21, ...), custom_call_target="tpu_custom_call" | custom-call | flops 1000 | bytes 1000 | tf_op jit(solution)/shard_map/mixer/pallas_call | solution.py:92
  157.5 1.6 copy-done.7
  159.1 0.1 reduce_sum.9
  159.2 6.0 %collective-permute-start.16 = (f32[384]{0:T(512)S(1)}, f32[384]{0:T(512)S(1)}, u32[]{:S(2)}, u32[]{:S(2)}) collective-permute-start(f32[384]{0:T(512)S(1)} %reduce_sum.9), channel_id=1, source_target_pairs={{0,1},{1,0},{2,3},{3,2},{4,5},{5,4},{6,7},{7,6},{8,9},{9,8},{10,11... | collective-permute-start | bytes 4616 | tf_op jit(solution)/shard_map/ppermute | solution.py:495
  165.3 2.8 %collective-permute-start.17 = (f32[384]{0:T(512)S(1)}, f32[384]{0:T(512)S(1)}, u32[]{:S(2)}, u32[]{:S(2)}) collective-permute-start(f32[384]{0:T(512)S(1)} %reduce_sum.9), channel_id=1, source_target_pairs={{0,2},{1,3},{2,0},{3,1},{4,6},{5,7},{6,4},{7,5},{8,10},{9,11},{10,... | collective-permute-start | bytes 4616 | tf_op jit(solution)/shard_map/ppermute | solution.py:495
  168.0 0.5 collective-permute-start.18
  168.5 0.1 fusion
  168.6 1.0 pad_maximum_fusion.2
  169.6 3.0 %collective-permute-done.18 = f32[384]{0:T(512)S(1)} collective-permute-done((f32[384]{0:T(512)S(1)}, f32[384]{0:T(512)S(1)}, u32[]{:S(2)}, u32[]{:S(2)}) %collective-permute-start.18) | collective-permute-done | bytes 1568 | tf_op jit(solution)/shard_map/ppermute | solution.py:495
  172.6 1.5 multiply_convert_fusion
  (54 shorter events, 0.1 us)
Async XLA Ops:
  15.3 23.2 %copy-start.30 = (bf16[384,512]{1,0:T(8,128)(2,1)S(1)}, bf16[384,512]{1,0:T(8,128)(2,1)}, u32[]{:S(2)}) copy-start(bf16[384,512]{1,0:T(8,128)(2,1)} %get-tuple-element.46) | copy-start | bytes 1179652
  15.3 6.1 %collective-permute-start.1 = (bf16[384,256]{1,0:T(8,128)(2,1)}, bf16[384,256]{1,0:T(8,128)(2,1)S(1)}, u32[]{:S(2)}, u32[]{:S(2)}) collective-permute-start(bf16[384,256]{1,0:T(8,128)(2,1)} %get-tuple-element.38), channel_id=1, source_target_pairs={{0,64},{4,68},{8,72},{12,76},{16,80},{20,84},{24,88},{28,92},{32,9... | collective-permute-start | bytes 589832 | tf_op jit(solution)/shard_map/ppermute | solution.py:441
  21.3 7.6 %collective-permute-start.2 = (bf16[384,256]{1,0:T(8,128)(2,1)}, bf16[384,256]{1,0:T(8,128)(2,1)S(1)}, u32[]{:S(2)}, u32[]{:S(2)}) collective-permute-start(bf16[384,256]{1,0:T(8,128)(2,1)} %get-tuple-element.38), channel_id=1, source_target_pairs={{0,16},{4,20},{8,24},{12,28},{16,32},{20,36},{24,40},{28,44},{32,4... | collective-permute-start | bytes 589832 | tf_op jit(solution)/shard_map/ppermute | solution.py:441
  23.0 6.2 %collective-permute-start.3 = (bf16[384,256]{1,0:T(8,128)(2,1)}, bf16[384,256]{1,0:T(8,128)(2,1)S(1)}, u32[]{:S(2)}, u32[]{:S(2)}) collective-permute-start(bf16[384,256]{1,0:T(8,128)(2,1)} %get-tuple-element.38), channel_id=1, source_target_pairs={{0,48},{4,52},{8,56},{12,60},{16,0},{20,4},{24,8},{28,12},{32,16},... | collective-permute-start | bytes 589832 | tf_op jit(solution)/shard_map/ppermute | solution.py:441
  25.1 9.0 %collective-permute-start.4 = (bf16[384,256]{1,0:T(8,128)(2,1)}, bf16[384,256]{1,0:T(8,128)(2,1)S(1)}, u32[]{:S(2)}, u32[]{:S(2)}) collective-permute-start(bf16[384,256]{1,0:T(8,128)(2,1)} %get-tuple-element.38), channel_id=1, source_target_pairs={{0,32},{4,36},{8,40},{12,44},{16,48},{20,52},{24,56},{28,60},{32,0... | collective-permute-start | bytes 589832 | tf_op jit(solution)/shard_map/ppermute | solution.py:441
  26.4 7.7 %collective-permute-start.5 = (bf16[384,256]{1,0:T(8,128)(2,1)S(1)}, bf16[384,256]{1,0:T(8,128)(2,1)S(1)}, u32[]{:S(2)}, u32[]{:S(2)}) collective-permute-start(bf16[384,256]{1,0:T(8,128)(2,1)S(1)} %collective-permute-done.1), channel_id=1, source_target_pairs={{0,4},{4,8},{8,12},{12,0},{16,20},{20,24},{24,28},{28,16},{32,36},... | collective-permute-start | bytes 589832 | tf_op jit(solution)/shard_map/ppermute | solution.py:441
  27.4 6.7 %collective-permute-start.6 = (bf16[384,256]{1,0:T(8,128)(2,1)S(1)}, bf16[384,256]{1,0:T(8,128)(2,1)S(1)}, u32[]{:S(2)}, u32[]{:S(2)}) collective-permute-start(bf16[384,256]{1,0:T(8,128)(2,1)S(1)} %collective-permute-done.1), channel_id=1, source_target_pairs={{0,12},{4,0},{8,4},{12,8},{16,28},{20,16},{24,20},{28,24},{32,44},... | collective-permute-start | bytes 589832 | tf_op jit(solution)/shard_map/ppermute | solution.py:441
  29.0 7.1 %collective-permute-start.7 = (bf16[384,256]{1,0:T(8,128)(2,1)S(1)}, bf16[384,256]{1,0:T(8,128)(2,1)S(1)}, u32[]{:S(2)}, u32[]{:S(2)}) collective-permute-start(bf16[384,256]{1,0:T(8,128)(2,1)S(1)} %collective-permute-done.1), channel_id=1, source_target_pairs={{0,8},{4,12},{8,0},{12,4},{16,24},{20,28},{24,16},{28,20},{32,40},... | collective-permute-start | bytes 589832 | tf_op jit(solution)/shard_map/ppermute | solution.py:441
  34.1 3.0 %copy-start.17 = (bf16[384,256]{1,0:T(8,128)(2,1)}, bf16[384,256]{1,0:T(8,128)(2,1)S(1)}, u32[]{:S(2)}) copy-start(bf16[384,256]{1,0:T(8,128)(2,1)S(1)} %collective-permute-done.6) | copy-start | bytes 589828
  36.1 2.3 %copy-start.19 = (bf16[384,256]{1,0:T(8,128)(2,1)}, bf16[384,256]{1,0:T(8,128)(2,1)S(1)}, u32[]{:S(2)}) copy-start(bf16[384,256]{1,0:T(8,128)(2,1)S(1)} %collective-permute-done.7) | copy-start | bytes 589828
  37.1 0.7 copy-start.15
  37.8 5.8 %copy-start.14 = (bf16[384,256]{1,0:T(8,128)(2,1)S(1)}, bf16[384,256]{1,0:T(8,128)(2,1)}, u32[]{:S(2)}) copy-start(bf16[384,256]{1,0:T(8,128)(2,1)} %get-tuple-element.38) | copy-start | bytes 589828
  37.8 38.7 %collective-permute-start.13 = (bf16[4,384,256]{2,1,0:T(8,128)(2,1)}, bf16[4,384,256]{2,1,0:T(8,128)(2,1)}, u32[]{:S(2)}, u32[]{:S(2)}) collective-permute-start(bf16[4,384,256]{2,1,0:T(8,128)(2,1)} %pad_maximum_fusion.1), channel_id=1, source_target_pairs={{0,16},{4,20},{8,24},{12,28},{16,32},{20,36},{24,40},{28,44},{32,4... | collective-permute-start | bytes 2359304 | tf_op jit(solution)/shard_map/ppermute | solution.py:441
  38.5 11.7 %collective-permute-start.8 = (bf16[384,512]{1,0:T(8,128)(2,1)S(1)}, bf16[384,512]{1,0:T(8,128)(2,1)S(1)}, u32[]{:S(2)}, u32[]{:S(2)}) collective-permute-start(bf16[384,512]{1,0:T(8,128)(2,1)S(1)} %copy-done.30), channel_id=1, source_target_pairs={{124,0},{120,4},{116,8},{112,12},{108,16},{104,20},{100,24},{96,28... | collective-permute-start | bytes 1179656 | tf_op jit(solution)/shard_map/ppermute | solution.py:474
  39.7 43.1 %collective-permute-start.14 = (bf16[4,384,256]{2,1,0:T(8,128)(2,1)}, bf16[4,384,256]{2,1,0:T(8,128)(2,1)}, u32[]{:S(2)}, u32[]{:S(2)}) collective-permute-start(bf16[4,384,256]{2,1,0:T(8,128)(2,1)} %pad_maximum_fusion.1), channel_id=1, source_target_pairs={{0,48},{4,52},{8,56},{12,60},{16,0},{20,4},{24,8},{28,12},{32,16},... | collective-permute-start | bytes 2359304 | tf_op jit(solution)/shard_map/ppermute | solution.py:441
  43.6 9.5 %copy-start = (bf16[2,256,1536]{2,1,0:T(8,128)(2,1)S(1)}, bf16[2,256,1536]{2,1,0:T(8,128)(2,1)}, u32[]{:S(2)}) copy-start(bf16[2,256,1536]{2,1,0:T(8,128)(2,1)} %turn_queries.2.refs_9_.refs_5_.refs_3_) | copy-start | bytes 4718596
  43.6 9.5 %copy-start.26 = (s32[32,69]{1,0:T(8,128)S(1)}, s32[32,69]{1,0:T(8,128)}, u32[]{:S(2)}) copy-start(s32[32,69]{1,0:T(8,128)} %constant.23.clone.refs_0_) | copy-start | bytes 26500
  44.5 41.1 %collective-permute-start.11 = (bf16[4,384,256]{2,1,0:T(8,128)(2,1)}, bf16[4,384,256]{2,1,0:T(8,128)(2,1)}, u32[]{:S(2)}, u32[]{:S(2)}) collective-permute-start(bf16[4,384,256]{2,1,0:T(8,128)(2,1)} %pad_maximum_fusion), channel_id=1, source_target_pairs={{0,4},{4,8},{8,12},{12,0},{16,20},{20,24},{24,28},{28,16},{32,36},... | collective-permute-start | bytes 2359304 | tf_op jit(solution)/shard_map/ppermute | solution.py:441
  46.5 39.1 %collective-permute-start.12 = (bf16[4,384,256]{2,1,0:T(8,128)(2,1)}, bf16[4,384,256]{2,1,0:T(8,128)(2,1)}, u32[]{:S(2)}, u32[]{:S(2)}) collective-permute-start(bf16[4,384,256]{2,1,0:T(8,128)(2,1)} %pad_maximum_fusion), channel_id=1, source_target_pairs={{0,12},{4,0},{8,4},{12,8},{16,28},{20,16},{24,20},{28,24},{32,44},... | collective-permute-start | bytes 2359304 | tf_op jit(solution)/shard_map/ppermute | solution.py:441
  50.2 0.8 copy-start.27
  53.0 1.1 copy-start.2
  54.2 0.9 copy-start.16
  55.1 0.9 copy-start.18
  56.0 0.9 copy-start.20
  75.8 0.6 copy-start.22
  76.5 9.2 %copy-start.3 = (bf16[1,256,1536]{2,1,0:T(8,128)(2,1)S(1)}, bf16[1,256,1536]{2,1,0:T(8,128)(2,1)}, u32[]{:S(2)}) copy-start(bf16[1,256,1536]{2,1,0:T(8,128)(2,1)} %turn_queries.3.refs_10_.refs_6_.refs_4_) | copy-start | bytes 2359300
  76.5 9.2 %copy-start.23 = (f32[1,8,1536]{2,1,0:T(8,128)S(1)}, f32[1,8,1536]{2,1,0:T(8,128)}, u32[]{:S(2)}) copy-start(f32[1,8,1536]{2,1,0:T(8,128)} %copy-done.22) | copy-start | bytes 147460
  76.5 9.2 %copy-start.25 = (s32[32,117]{1,0:T(8,128)S(1)}, s32[32,117]{1,0:T(8,128)}, u32[]{:S(2)}) copy-start(s32[32,117]{1,0:T(8,128)} %constant.24.clone.refs_0_) | copy-start | bytes 44932
  76.5 31.6 %collective-permute-start.10 = (bf16[4,384,256]{2,1,0:T(8,128)(2,1)}, bf16[4,384,256]{2,1,0:T(8,128)(2,1)S(1)}, u32[]{:S(2)}, u32[]{:S(2)}) collective-permute-start(bf16[4,384,256]{2,1,0:T(8,128)(2,1)} %pad_maximum_fusion.1), channel_id=1, source_target_pairs={{0,32},{4,36},{8,40},{12,44},{16,48},{20,52},{24,56},{28,60},{32,0... | collective-permute-start | bytes 2359304 | tf_op jit(solution)/shard_map/ppermute | solution.py:441
  76.5 31.6 %collective-permute-start.9 = (bf16[4,384,256]{2,1,0:T(8,128)(2,1)}, bf16[4,384,256]{2,1,0:T(8,128)(2,1)S(1)}, u32[]{:S(2)}, u32[]{:S(2)}) collective-permute-start(bf16[4,384,256]{2,1,0:T(8,128)(2,1)} %pad_maximum_fusion), channel_id=1, source_target_pairs={{0,8},{4,12},{8,0},{12,4},{16,24},{20,28},{24,16},{28,20},{32,40},... | collective-permute-start | bytes 2359304 | tf_op jit(solution)/shard_map/ppermute | solution.py:441
  82.8 26.2 %copy-start.1 = (bf16[2,256,1536]{2,1,0:T(8,128)(2,1)S(1)}, bf16[2,256,1536]{2,1,0:T(8,128)(2,1)}, u32[]{:S(2)}) copy-start(bf16[2,256,1536]{2,1,0:T(8,128)(2,1)} %turn_queries.2.refs_9_.refs_5_.refs_3_) | copy-start | bytes 4718596
  82.8 26.2 %copy-start.24 = (s32[32,69]{1,0:T(8,128)S(1)}, s32[32,69]{1,0:T(8,128)}, u32[]{:S(2)}) copy-start(s32[32,69]{1,0:T(8,128)} %constant.25.clone.refs_0_) | copy-start | bytes 26500
  82.8 48.5 %collective-permute-start = (bf16[176,2048]{1,0:T(8,128)(2,1)}, bf16[176,2048]{1,0:T(8,128)(2,1)}, u32[]{:S(2)}, u32[]{:S(2)}) collective-permute-start(bf16[176,2048]{1,0:T(8,128)(2,1)} %mixed_tail.1), channel_id=1, source_target_pairs={{0,4},{4,8},{8,12},{12,16},{16,20},{20,24},{24,28},{28,32},{32,36}... | collective-permute-start | bytes 2162696 | tf_op jit(solution)/shard_map/ppermute | solution.py:482
  108.1 0.9 copy-start.10
  109.0 1.1 copy-start.11
  110.1 21.0 %copy-start.28 = (bf16[128,128]{1,0:T(8,128)(2,1)S(1)}, bf16[128,128]{1,0:T(8,128)(2,1)}, u32[]{:S(2)}) copy-start(bf16[128,128]{1,0:T(8,128)(2,1)} %param.17) | copy-start | bytes 98308
  110.1 21.1 %copy-start.29 = (bf16[2048]{0:T(1024)(128)(2,1)S(1)}, bf16[2048]{0:T(1024)(128)(2,1)}, u32[]{:S(2)}) copy-start(bf16[2048]{0:T(1024)(128)(2,1)} %param.19) | copy-start | bytes 12292
  110.1 21.2 %copy-start.4 = (bf16[384,2048]{1,0:T(8,128)(2,1)S(1)}, bf16[384,2048]{1,0:T(8,128)(2,1)}, u32[]{:S(2)}) copy-start(bf16[384,2048]{1,0:T(8,128)(2,1)} %one.3) | copy-start | bytes 4718596
  110.1 21.2 %copy-start.21 = (bf16[3,7,2048]{2,1,0:T(8,128)(2,1)S(1)}, bf16[3,7,2048]{2,1,0:T(8,128)(2,1)}, u32[]{:S(2)}) copy-start(bf16[3,7,2048]{2,1,0:T(8,128)(2,1)} %taps.3) | copy-start | bytes 258052
  128.9 0.9 copy-start.12
  129.8 29.4 %collective-permute-start.15 = (bf16[384,512]{1,0:T(8,128)(2,1)}, bf16[384,512]{1,0:T(8,128)(2,1)S(1)}, u32[]{:S(2)}, u32[]{:S(2)}) collective-permute-start(bf16[384,512]{1,0:T(8,128)(2,1)} %get-tuple-element.61), channel_id=1, source_target_pairs={{0,124},{4,120},{8,116},{12,112},{16,108},{20,104},{24,100},{28,96... | collective-permute-start | bytes 1179656 | tf_op jit(solution)/shard_map/ppermute | solution.py:490
  131.4 1.4 copy-start.5
  132.8 1.4 copy-start.6
  134.2 1.4 copy-start.9
  135.6 32.9 %copy-start.13 = (bf16[384,1024]{1,0:T(8,128)(2,1)S(1)}, bf16[384,1024]{1,0:T(8,128)(2,1)}, u32[]{:S(2)}) copy-start(bf16[384,1024]{1,0:T(8,128)(2,1)} %copy-done.12) | copy-start | bytes 2359300
  157.5 1.6 copy-start.7
  159.2 10.3 %collective-permute-start.16 = (f32[384]{0:T(512)S(1)}, f32[384]{0:T(512)S(1)}, u32[]{:S(2)}, u32[]{:S(2)}) collective-permute-start(f32[384]{0:T(512)S(1)} %reduce_sum.9), channel_id=1, source_target_pairs={{0,1},{1,0},{2,3},{3,2},{4,5},{5,4},{6,7},{7,6},{8,9},{9,8},{10,11... | collective-permute-start | bytes 4616 | tf_op jit(solution)/shard_map/ppermute | solution.py:495
  165.3 4.3 %collective-permute-start.17 = (f32[384]{0:T(512)S(1)}, f32[384]{0:T(512)S(1)}, u32[]{:S(2)}, u32[]{:S(2)}) collective-permute-start(f32[384]{0:T(512)S(1)} %reduce_sum.9), channel_id=1, source_target_pairs={{0,2},{1,3},{2,0},{3,1},{4,6},{5,7},{6,4},{7,5},{8,10},{9,11},{10,... | collective-permute-start | bytes 4616 | tf_op jit(solution)/shard_map/ppermute | solution.py:495
  168.0 4.5 %collective-permute-start.18 = (f32[384]{0:T(512)S(1)}, f32[384]{0:T(512)S(1)}, u32[]{:S(2)}, u32[]{:S(2)}) collective-permute-start(f32[384]{0:T(512)S(1)} %reduce_sum.9), channel_id=1, source_target_pairs={{0,3},{1,2},{2,1},{3,0},{4,7},{5,6},{6,5},{7,4},{8,11},{9,10},{10,... | collective-permute-start | bytes 4616 | tf_op jit(solution)/shard_map/ppermute | solution.py:495
  168.5 4.1 %copy-start.8 = (f32[384,2048]{1,0:T(8,128)S(1)}, f32[384,2048]{1,0:T(8,128)}, u32[]{:S(2)}) copy-start(f32[384,2048]{1,0:T(8,128)} %copy-done.7) | copy-start | bytes 9437188
where the time goes:
time: 175 us; the launch traced here: 174 us
  Pallas kernels  105 us (60%)
  starting transfers between devices  28.9 us (17%)
  waiting for transfers between devices  19.4 us (11%)
  local copies, waits for them, and re-layouts  14.9 us (9%)
  other arithmetic  4.66 us (3%)
    pallas_call x3, Pallas kernels, attend_call(): pl.pallas_call(functools.partial(attend_kernel, sizes, groups, starts, la...  60 us
    pallas_call x1, Pallas kernels, mixer_call(): pl.pallas_call(mixer_kernel, grid=(width // LANES,), in_specs=[spec] * 3...  21.9 us
    unnamed x62, local copies, waits for them, and re-layouts  14.7 us
    pallas_call x1, Pallas kernels, pack_call(): pl.pallas_call(pack_kernel, in_specs=[vmem, vmem, hbm], out_specs=[vmem,...  14.6 us
    ppermute x13, starting transfers between devices, moved(): lax.ppermute(value, 'ctx', [(i, neighbour(i, x, z, y)) for i in range(BLO...  14.2 us
    ppermute x13, waiting for transfers between devices, moved(): lax.ppermute(value, 'ctx', [(i, neighbour(i, x, z, y)) for i in range(BLO...  12.8 us
    ppermute x3, starting transfers between devices, shards(): lax.ppermute(sums, 'tp', [(i, i ^ step) for i in range(4)])  9.25 us
    pallas_call x2, Pallas kernels, turn_call(): pl.pallas_call(turn_kernel, grid=(quads,), in_specs=[pl.BlockSpec((rows,...  4.46 us
  transfers between devices with their start and end apart: 19, of which 6 were waited for; matrix products, arithmetic and copies ran while one was open for 1% of the time, Pallas kernels for 52%

commit v1 on v0

--- a/solution.py
+++ b/solution.py
@@ -11,95 +11,110 @@
 
 f32=jnp.float32; bf=jnp.bfloat16
 SHORT=7; GROUP=16; LANES=128; EDGE=16; TAPS=128; BLK=64
+VMEM = 60 * 2**20
+ATTEND_VMEM = 28 * 2**20
 LIGHT = pl.CostEstimate(flops=1000, bytes_accessed=1000, transcendentals=0)
-
-def tail_kernel(one, two, val, taps, out, x_scr):
+PARAMS = pltpu.CompilerParams(vmem_limit_bytes=VMEM)
+
+def tail_kernel(one, two, val, taps, out, streams, x_scr, sems):
     keep = TAPS
-    last = one.shape[0]
+    first = one.shape[0] - keep - EDGE
+    copies = [pltpu.make_async_copy(ref.at[first:], streams.at[n], sems.at[n]) for n, ref in enumerate((one, val, two))]
+    for copy in copies:
+        copy.start()
+    for copy in copies:
+        copy.wait()
     for lanes in range(one.shape[1] // LANES):
         c = slice(lanes * LANES, (lanes + 1) * LANES)
         t = taps[:, :, c].astype(f32)
 
-        def short(ref, which, slot):
-            x_scr[slot] = ref[last - keep - EDGE:, c].astype(f32)
+        def short(stream, which, slot):
+            x_scr[slot] = streams[stream, :, c].astype(f32)
             total = t[which, 0:1] * x_scr[slot, EDGE:EDGE + keep, :]
             for j in range(1, SHORT):
                 total += t[which, j:j + 1] * x_scr[slot, EDGE - j:EDGE - j + keep, :]
             return total
-        out[0:keep, c] = (short(one, 0, 2 * (lanes % 2)) * short(val, 2, 2 * (lanes % 2) + 1)).astype(bf)
-    for n, ref in enumerate((one, two, val)):
-        out[keep + EDGE * n:keep + EDGE * (n + 1)] = ref[last - EDGE:, :]
+        slot = 2 * (lanes % 4)
+        out[0:keep, c] = (short(0, 0, slot) * short(1, 2, slot + 1)).astype(bf)
+    for n, stream in enumerate((0, 2, 1)):
+        out[keep + EDGE * n:keep + EDGE * (n + 1)] = streams[stream, keep:]
 
 
 def tail_call(one, two, val, taps):
     rows, width = one.shape
-    tile = 4 * LANES
-    spec = pl.BlockSpec((rows // 2, tile), lambda i: (1, i))
-    out_rows = TAPS + 3 * EDGE
-    return pl.pallas_call(tail_kernel, grid=(width // tile,),
-        in_specs=[spec] * 3 + [pl.BlockSpec((3, SHORT, tile), lambda i: (0, 0, i))],
-        out_specs=pl.BlockSpec((out_rows, tile), lambda i: (0, i)),
-        out_shape=jax.ShapeDtypeStruct((out_rows, width), bf),
-        scratch_shapes=[pltpu.VMEM((4, TAPS + EDGE, LANES), f32)],
+    hbm = pl.BlockSpec(memory_space=pltpu.HBM)
+    vmem = pl.BlockSpec(memory_space=pltpu.VMEM)
+    return pl.pallas_call(tail_kernel, in_specs=[hbm] * 3 + [vmem], out_specs=vmem,
+        out_shape=jax.ShapeDtypeStruct((TAPS + 3 * EDGE, width), bf),
+        scratch_shapes=[pltpu.VMEM((3, TAPS + EDGE, width), bf), pltpu.VMEM((8, TAPS + EDGE, LANES), f32),
+                        pltpu.SemaphoreType.DMA((3,))],
+        compiler_params=pltpu.CompilerParams(vmem_limit_bytes=ATTEND_VMEM),
         cost_estimate=LIGHT,
         name="mixed_tail")(one, two, val, taps)
 
 
 def mixer_kernel(one, two, val, halo, taps, rev, res, branch, squares, x_scr, m_scr, t_scr):
     rows = one.shape[0]
-    t = taps[...].astype(f32)
-    def short(ref, n):
-        lo = TAPS + EDGE * n
-        x_scr[n, 0:EDGE] = halo[lo:lo + EDGE, :].astype(f32)
-        x_scr[n, EDGE:] = ref[...].astype(f32)
-        total = t[n, 0:1] * x_scr[n, EDGE:, :]
-        for j in range(1, SHORT):
-            total += t[n, j:j + 1] * x_scr[n, EDGE - j:EDGE - j + rows, :]
-        return total
-    m_scr[0:TAPS] = halo[0:TAPS]
-    m_scr[TAPS:] = (short(one, 0) * short(val, 2)).astype(bf)
-    gate = short(two, 1)
     groups = LANES // GROUP
-    for g in range(groups):
-        row = jnp.broadcast_to(rev[g:g + 1, :], (BLK, 2 * TAPS))
-        rolled = pltpu.roll(row, 0, 1, stride=1, stride_axis=0)
-        t_scr[g * BLK:(g + 1) * BLK] = rolled.astype(bf)
+    span = BLK + TAPS
     lane = lax.broadcasted_iota(jnp.int32, (BLK, LANES), 1) // GROUP
-    span = BLK + TAPS
-    total = jnp.zeros((8, 128), f32)
-    for pair in range(rows // (2 * BLK)):
-        at = 2 * BLK * pair
-        window = jnp.concatenate([m_scr[at:at + span], m_scr[at + BLK:at + BLK + span]], axis=1)
-        wide = jnp.dot(t_scr[:, :span], window, preferred_element_type=f32)
-        for half in range(2):
-            r = slice(at + BLK * half, at + BLK * (half + 1))
-            c = slice(LANES * half, LANES * (half + 1))
-            medium = wide[0:BLK, c]
-            for g in range(1, groups):
-                medium = jnp.where(lane == g, wide[g * BLK:(g + 1) * BLK, c], medium)
-            summed = res[r].astype(f32) + gate[r] * medium
-            branch[r] = summed
-            sq = summed * summed
-            @pl.when(pl.program_id(0) == 0)
-            def _(): squares[r] = sq
-            @pl.when(pl.program_id(0) > 0)
-            def _(): squares[r] += sq
+    for unit in range(one.shape[1] // LANES):
+        lanes = slice(unit * LANES, (unit + 1) * LANES)
+        t = taps[:, :, lanes].astype(f32)
+
+        def short(ref, n):
+            lo = TAPS + EDGE * n
+            x_scr[unit, n, 0:EDGE] = halo[lo:lo + EDGE, lanes].astype(f32)
+            x_scr[unit, n, EDGE:] = ref[:, lanes].astype(f32)
+            total = t[n, 0:1] * x_scr[unit, n, EDGE:, :]
+            for j in range(1, SHORT):
+                total += t[n, j:j + 1] * x_scr[unit, n, EDGE - j:EDGE - j + rows, :]
+            return total
+        m_scr[unit, 0:TAPS] = halo[0:TAPS, lanes]
+        m_scr[unit, TAPS:] = (short(one, 0) * short(val, 2)).astype(bf)
+        gate = short(two, 1)
+        for g in range(groups):
+            row = jnp.broadcast_to(rev[unit * groups + g:unit * groups + g + 1, :], (BLK, 2 * TAPS))
+            rolled = pltpu.roll(row, 0, 1, stride=1, stride_axis=0)
+            t_scr[unit, g * BLK:(g + 1) * BLK] = rolled.astype(bf)
+        for pair in range(rows // (2 * BLK)):
+            at = 2 * BLK * pair
+            window = jnp.concatenate([m_scr[unit, at:at + span], m_scr[unit, at + BLK:at + BLK + span]], axis=1)
+            wide = jnp.dot(t_scr[unit, :, :span], window, preferred_element_type=f32)
+            for half in range(2):
+                r = slice(at + BLK * half, at + BLK * (half + 1))
+                c = slice(LANES * half, LANES * (half + 1))
+                medium = wide[0:BLK, c]
+                for g in range(1, groups):
+                    medium = jnp.where(lane == g, wide[g * BLK:(g + 1) * BLK, c], medium)
+                summed = res[r, lanes].astype(f32) + gate[r] * medium
+                branch[r, lanes] = summed
+                square = summed * summed
+                if unit == 0:
+                    square += jnp.where(pl.program_id(0) == 0, 0.0, squares[r])
+                else:
+                    square += squares[r]
+                squares[r] = square
+
 
 def mixer_call(one, two, val, halo, taps, rev, res):
     rows, width = one.shape
-    spec = pl.BlockSpec((rows, LANES), lambda i: (0, i))
-    groups = LANES // GROUP
-    return pl.pallas_call(mixer_kernel, grid=(width // LANES,),
-        in_specs=[spec] * 3 + [pl.BlockSpec((halo.shape[0], LANES), lambda i: (0, i)),
-            pl.BlockSpec((3, SHORT, LANES), lambda i: (0, 0, i)),
+    units = 4
+    tile = units * LANES
+    groups = tile // GROUP
+    spec = pl.BlockSpec((rows, tile), lambda i: (0, i))
+    return pl.pallas_call(mixer_kernel, grid=(width // tile,),
+        in_specs=[spec] * 3 + [pl.BlockSpec((halo.shape[0], tile), lambda i: (0, i)),
+            pl.BlockSpec((3, SHORT, tile), lambda i: (0, 0, i)),
             pl.BlockSpec((groups, 2 * TAPS), lambda i: (i, 0)), spec],
         out_specs=[spec, pl.BlockSpec((rows, LANES), lambda i: (0, 0))],
         out_shape=[jax.ShapeDtypeStruct((rows, width), f32), jax.ShapeDtypeStruct((rows, LANES), f32)],
-        scratch_shapes=[pltpu.VMEM((3, EDGE + rows, LANES), f32), pltpu.VMEM((TAPS + rows, LANES), bf),
-            pltpu.VMEM((groups * BLK, 2 * TAPS), bf)],
-        compiler_params=pltpu.CompilerParams(vmem_limit_bytes=32 * 2**20),
+        scratch_shapes=[pltpu.VMEM((units, 3, EDGE + rows, LANES), f32), pltpu.VMEM((units, TAPS + rows, LANES), bf),
+            pltpu.VMEM((units, LANES // GROUP * BLK, 2 * TAPS), bf)],
+        compiler_params=PARAMS,
         cost_estimate=LIGHT,
         name="mixer")(one, two, val, halo, taps, rev, res)
+
 
 def reversed_taps(filters):
     flipped = filters.astype(f32)[:, ::-1]
@@ -114,24 +129,23 @@
 SCALE = math.log2(math.e) / math.sqrt(HD)
 
 
-def pack_kernel(keys, values, queries, packed, given, sem):
-    middle = given.shape[1]
-    copy = pltpu.make_async_copy(queries.at[:, middle:], given, sem)
-    copy.start()
+def pack_kernel(keys, values, queries, packed, given):
     packed[:, :HD] = keys[...]
     turned = values[...].astype(f32).T.astype(bf)
     for part in range(values.shape[0] // HD):
         packed[part * HD:(part + 1) * HD, HD:] = turned[:, part * HD:(part + 1) * HD]
-    copy.wait()
+    given[...] = queries[...]
 
 
 def pack_call(keys, values, queries):
-    hbm = pl.BlockSpec(memory_space=pltpu.HBM)
-    vmem = pl.BlockSpec(memory_space=pltpu.VMEM)
-    return pl.pallas_call(pack_kernel, in_specs=[vmem, vmem, hbm], out_specs=[vmem, hbm],
-                          out_shape=[jax.ShapeDtypeStruct((keys.shape[0], 2 * HD), bf),
-                                     jax.ShapeDtypeStruct((queries.shape[0], queries.shape[1] // 2), bf)],
-                          scratch_shapes=[pltpu.SemaphoreType.DMA], name="pack_keys")(keys, values, queries)
+    rows, width = queries.shape
+    shape = (rows, width // 2)
+    whole = lambda i: (0, 0)
+    return pl.pallas_call(pack_kernel, grid=(1,),
+        in_specs=[pl.BlockSpec(keys.shape, whole), pl.BlockSpec(values.shape, whole), pl.BlockSpec(shape, lambda i: (0, 1))],
+        out_specs=[pl.BlockSpec((rows, 2 * HD), whole), pl.BlockSpec(shape, whole)],
+        out_shape=[jax.ShapeDtypeStruct((rows, 2 * HD), bf), jax.ShapeDtypeStruct(shape, bf)],
+        compiler_params=PARAMS, cost_estimate=LIGHT, name="pack_keys")(keys, values, queries)
 
 
 def turn_kernel(queries, turned):
@@ -151,7 +165,7 @@
         in_specs=[pl.BlockSpec((rows, QUAD * HD), lambda i: (0, i))],
         out_specs=pl.BlockSpec((1, 2 * HD, QUAD * rows), lambda i: (i, 0, 0)),
         out_shape=jax.ShapeDtypeStruct((quads, 2 * HD, QUAD * rows), bf),
-        cost_estimate=LIGHT,
+        compiler_params=pltpu.CompilerParams(vmem_limit_bytes=ATTEND_VMEM), cost_estimate=LIGHT,
         name="turn_queries")(queries)
 
 
@@ -251,18 +265,13 @@
     @pl.loop(0, n_slow)
     def _(number):
         quad, block, *modes = decode(table[me, at_slow + number])
+        lead = (lax.broadcasted_iota(jnp.int32, (rows, rows), 0) - lax.broadcasted_iota(jnp.int32, (rows, rows), 1))
+        lead = jnp.concatenate([lead, lead], axis=1)
+        limits = [jnp.where(mode == FULL, rows, jnp.where(mode == DIAGONAL, 0, -2 * rows)) for mode in modes]
         for pair in range(2):
-            s_scr[...] = multiply_keys(quad, block, pair)
-            key = lax.broadcasted_iota(jnp.int32, (rows, rows), 0)
-            query = lax.broadcasted_iota(jnp.int32, (rows, rows), 1)
-            for part, mode in enumerate(modes):
-                limit = jnp.where(mode == FULL, rows, jnp.where(mode == DIAGONAL, 0, -2 * rows))
-                allowed = key - query <= limit
-                for head in range(2):
-                    r = slice(part * rows, (part + 1) * rows)
-                    c = slice(head * rows, (head + 1) * rows)
-                    s_scr[r, c] = jnp.where(allowed, s_scr[r, c], -1e30)
-            weights, factor = soften(quad, pair, s_scr[...])
+            s = multiply_keys(quad, block, pair)
+            s = jnp.concatenate([jnp.where(lead <= limits[n], s[n * rows:(n + 1) * rows], -1e30) for n in range(2)], axis=0)
+            weights, factor = soften(quad, pair, s)
             multiply_values(quad, block, pair, weights, factor)
 
     def fast_entry(number):
@@ -306,7 +315,7 @@
             for quad in range(count):
                 for head in range(QUAD):
                     c = slice(head * rows, (head + 1) * rows)
-                    value = acc[at + quad, :HD, c] / acc[at + quad, HD:HD + 1, c]
+                    value = acc[at + quad, :HD, c] * (1.0 / acc[at + quad, HD:HD + 1, c])
                     to = (quad * QUAD + head) * HD
                     results[n][:, to:to + HD] = value.T.astype(bf)
             at += count
@@ -334,6 +343,7 @@
     quads = sum(groups)
     starts = tuple(state is None for state in states)
     hbm = pl.BlockSpec(memory_space=pltpu.HBM)
+    anywhere = pl.BlockSpec(memory_space=pl.ANY)
     operands = [table, *pieces, *turned] + [part for state in states if state is not None for part in state]
     if last:
         out_shape = [jax.ShapeDtypeStruct((rows, count * QUAD * HD), bf) for count in groups]
@@ -346,7 +356,7 @@
         out_specs = [hbm] * len(out_shape)
     result = pl.pallas_call(
         functools.partial(attend_kernel, sizes, groups, starts, last, rows),
-        in_specs=[pl.BlockSpec(memory_space=pltpu.SMEM)] + [hbm] * (len(operands) - 1),
+        in_specs=[pl.BlockSpec(memory_space=pltpu.SMEM)] + [anywhere] * len(pieces) + [hbm] * (len(operands) - 1 - len(pieces)),
         out_specs=out_specs,
         out_shape=out_shape,
         scratch_shapes=[
@@ -361,7 +371,7 @@
             pltpu.SemaphoreType.DMA((2 * shards,)),
             pltpu.SemaphoreType.DMA((2 * len(groups),)),
         ],
-        compiler_params=pltpu.CompilerParams(vmem_limit_bytes=48 * 2**20),
+        compiler_params=pltpu.CompilerParams(vmem_limit_bytes=ATTEND_VMEM),
         cost_estimate=LIGHT,
         name="attend",
     )(*operands)

time: 175 us -> 136 us (0.78)
  Pallas kernels: 105 us -> 78.8 us
  local copies, waits for them, and re-layouts: 14.9 us -> 1.78 us
  waiting for transfers between devices: 19.4 us -> 22 us
    pallas_call x3, Pallas kernels: 40.8 us -> 16.7 us  [the longest x1 12.2 us: mixer_call(): pl.pallas_call(mixer_kernel, grid=(width // tile,), in_specs=[spec] * 3 +...]
    unnamed x62 -> x28, local copies, waits for them, and re-layouts: 14.7 us -> 0.93 us
    pallas_call x2, Pallas kernels: 4.46 us -> 0.77 us  [turn_call(): pl.pallas_call(turn_kernel, grid=(quads,), in_specs=[pl.BlockSpec((rows,...]
    ppermute x1, waiting for transfers between devices: 3.64 us -> 6.18 us  [shards(): lax.ppermute(given, 'ctx', [(mirrored(i), i) for i in range(SHARED)])]
    another operation x2, other arithmetic: 1.97 us -> 0.2 us  [shards(): a_line, b_line = (jnp.stack(a), jnp.stack(b))]
  transfers between devices with their start and end apart: 19 -> 19, of which waited for: 6 -> 6; matrix products, arithmetic and copies ran while one was open for 1% -> 2% of each run, Pallas kernels for 52% -> 56%
where the time goes in v1:
time: 136 us
  Pallas kernels  78.8 us (58%)
  starting transfers between devices  28.8 us (21%)
  waiting for transfers between devices  22 us (16%)
  other arithmetic  3.82 us (3%)
  local copies, waits for them, and re-layouts  1.78 us (1%)
    pallas_call x3, Pallas kernels, attend_call(): pl.pallas_call(functools.partial(attend_kernel, sizes, groups, starts, la...  61.3 us
    ppermute x13, starting transfers between devices, moved(): lax.ppermute(value, 'ctx', [(i, neighbour(i, x, z, y)) for i in range(BLO...  14.4 us
    ppermute x13, waiting for transfers between devices, moved(): lax.ppermute(value, 'ctx', [(i, neighbour(i, x, z, y)) for i in range(BLO...  12.8 us
    pallas_call x1, Pallas kernels, mixer_call(): pl.pallas_call(mixer_kernel, grid=(width // tile,), in_specs=[spec] * 3 +...  12.2 us
    ppermute x3, starting transfers between devices, shards(): lax.ppermute(sums, 'tp', [(i, i ^ step) for i in range(4)])  9.35 us
    ppermute x1, waiting for transfers between devices, shards(): lax.ppermute(given, 'ctx', [(mirrored(i), i) for i in range(SHARED)])  6.18 us
    ppermute x3, waiting for transfers between devices, shards(): lax.ppermute(sums, 'tp', [(i, i ^ step) for i in range(4)])  2.98 us
  transfers between devices with their start and end apart: 19, of which 6 were waited for; matrix products, arithmetic and copies ran while one was open for 2% of the time, Pallas kernels for 56%

profile of v1, /device:TPU:17, one launch (start us, length us, event | category | flops | bytes accessed | tf_op | source)
XLA Modules:
  0.0 136.1 jit_solution(12747812065137455788)
XLA Ops:
  0.6 2.0 %pack_keys.1 = (bf16[384,256]{1,0:T(8,128)(2,1)}, bf16[384,512]{1,0:T(8,128)(2,1)}) custom-call(bf16[384,128]{1,0:T(8,128)(2,1)} %keys.1, bf16[384,128]{1,0:T(8,128)(2,1)} %values.1, bf16[384,1024]{1,0:T(8,128)(2,1)} %queries.3), custom_call_target="tpu_custom_call" | custom-call | flops 1000 | bytes 1000 | tf_op jit(solution)/shard_map/pack_keys/pallas_call | solution.py:144
  2.7 1.2 collective-permute-start.1
  3.9 4.8 %collective-permute-done.1 = bf16[384,256]{1,0:T(8,128)(2,1)S(1)} collective-permute-done((bf16[384,256]{1,0:T(8,128)(2,1)}, bf16[384,256]{1,0:T(8,128)(2,1)S(1)}, u32[]{:S(2)}, u32[]{:S(2)}) %collective-permute-start.1) | collective-permute-done | bytes 196640 | tf_op jit(solution)/shard_map/ppermute | solution.py:451
  8.6 1.6 %collective-permute-start.2 = (bf16[384,256]{1,0:T(8,128)(2,1)}, bf16[384,256]{1,0:T(8,128)(2,1)S(1)}, u32[]{:S(2)}, u32[]{:S(2)}) collective-permute-start(bf16[384,256]{1,0:T(8,128)(2,1)} %get-tuple-element.38), channel_id=1, source_target_pairs={{0,16},{4,20},{8,24},{12,28},{16,32},{20,36},{24,40},{28,44},{32,4... | collective-permute-start | bytes 589832 | tf_op jit(solution)/shard_map/ppermute | solution.py:451
  10.3 2.1 %collective-permute-start.3 = (bf16[384,256]{1,0:T(8,128)(2,1)}, bf16[384,256]{1,0:T(8,128)(2,1)S(1)}, u32[]{:S(2)}, u32[]{:S(2)}) collective-permute-start(bf16[384,256]{1,0:T(8,128)(2,1)} %get-tuple-element.38), channel_id=1, source_target_pairs={{0,48},{4,52},{8,56},{12,60},{16,0},{20,4},{24,8},{28,12},{32,16},... | collective-permute-start | bytes 589832 | tf_op jit(solution)/shard_map/ppermute | solution.py:451
  12.4 1.3 collective-permute-start.4
  13.7 1.0 collective-permute-start.5
  14.7 0.5 collective-permute-start.6
  15.2 1.1 collective-permute-done.2
  16.3 0.2 collective-permute-start.7
  16.5 0.0 collective-permute-done.3
  16.5 4.9 %collective-permute-done.4 = bf16[384,256]{1,0:T(8,128)(2,1)S(1)} collective-permute-done((bf16[384,256]{1,0:T(8,128)(2,1)}, bf16[384,256]{1,0:T(8,128)(2,1)S(1)}, u32[]{:S(2)}, u32[]{:S(2)}) %collective-permute-start.4) | collective-permute-done | bytes 196640 | tf_op jit(solution)/shard_map/ppermute | solution.py:451
  21.4 0.0 collective-permute-done.5
  21.4 0.0 collective-permute-done.6
  21.4 2.0 %collective-permute-done.7 = bf16[384,256]{1,0:T(8,128)(2,1)S(1)} collective-permute-done((bf16[384,256]{1,0:T(8,128)(2,1)S(1)}, bf16[384,256]{1,0:T(8,128)(2,1)S(1)}, u32[]{:S(2)}, u32[]{:S(2)}) %collective-permute-start.7) | collective-permute-done | bytes 196640 | tf_op jit(solution)/shard_map/ppermute | solution.py:451
  23.4 0.1 pad_maximum_fusion.1
  23.5 0.0 copy-start.4
  23.5 0.8 collective-permute-start.13
  24.3 1.3 collective-permute-start.8
  25.6 1.4 %collective-permute-start.14 = (bf16[4,384,256]{2,1,0:T(8,128)(2,1)S(1)}, bf16[4,384,256]{2,1,0:T(8,128)(2,1)S(1)}, u32[]{:S(2)}, u32[]{:S(2)}) collective-permute-start(bf16[4,384,256]{2,1,0:T(8,128)(2,1)S(1)} %pad_maximum_fusion.1), channel_id=1, source_target_pairs={{0,48},{4,52},{8,56},{12,60},{16,0},{20,4},{24,8},{28,12},{32,16},... | collective-permute-start | bytes 2359304 | tf_op jit(solution)/shard_map/ppermute | solution.py:451
  27.0 0.5 turn_queries.2.refs_9_.refs_5_.refs_3_
  27.6 0.0 copy-start.8
  27.6 0.1 pad_maximum_fusion
  27.7 2.1 %collective-permute-start.11 = (bf16[4,384,256]{2,1,0:T(8,128)(2,1)S(1)}, bf16[4,384,256]{2,1,0:T(8,128)(2,1)S(1)}, u32[]{:S(2)}, u32[]{:S(2)}) collective-permute-start(bf16[4,384,256]{2,1,0:T(8,128)(2,1)S(1)} %pad_maximum_fusion), channel_id=1, source_target_pairs={{0,4},{4,8},{8,12},{12,0},{16,20},{20,24},{24,28},{28,16},{32,36},... | collective-permute-start | bytes 2359304 | tf_op jit(solution)/shard_map/ppermute | solution.py:451
  29.8 0.0 collective-permute-start.12
  29.8 6.2 %collective-permute-done.8.queries = bf16[384,512]{1,0:T(8,128)(2,1)S(1)} collective-permute-done((bf16[384,512]{1,0:T(8,128)(2,1)S(1)}, bf16[384,512]{1,0:T(8,128)(2,1)S(1)}, u32[]{:S(2)}, u32[]{:S(2)}) %collective-permute-start.8) | collective-permute-done | bytes 393248 | tf_op jit(solution)/shard_map/ppermute | solution.py:484
  36.0 0.2 turn_queries.3.refs_10_.refs_6_.refs_4_
  36.2 0.0 copy-start
  36.2 0.0 copy-start.1
  36.2 0.0 copy-start.5
  36.2 18.9 %attend.3 = (f32[2,144,1536]{2,1,0:T(8,128)S(1)}, f32[2,8,1536]{2,1,0:T(8,128)S(1)}, f32[1,144,1536]{2,1,0:T(8,128)S(1)}, f32[1,8,1536]{2,1,0:T(8,128)S(1)}) custom-call(s32[32,69]{1,0:T(8,128)S(1)} %copy-done.8, bf16[1,384,256]{2,1,0:T(8,128)(2,1)S(1)} %bitcast.9, bf16[1,384,256]{2,1,0:T(8,128)(2,1)S(1)} %bitcast.13, bf16[1,384,256]{2,1,0:T(8,128)(2,1)S(1)} %bitcast.15, ...), custom_call_target="tpu_custom_call" | custom-call | flops 1000 | bytes 1000 | tf_op jit(solution)/shard_map/attend/pallas_call | solution.py:357
  55.2 0.0 copy-start.7
  55.2 0.1 collective-permute-start.10
  55.3 0.0 collective-permute-done.13.refs_3_
  55.3 2.1 %collective-permute-start.9 = (bf16[4,384,256]{2,1,0:T(8,128)(2,1)S(1)}, bf16[4,384,256]{2,1,0:T(8,128)(2,1)S(1)}, u32[]{:S(2)}, u32[]{:S(2)}) collective-permute-start(bf16[4,384,256]{2,1,0:T(8,128)(2,1)S(1)} %pad_maximum_fusion), channel_id=1, source_target_pairs={{0,8},{4,12},{8,0},{12,4},{16,24},{20,28},{24,16},{28,20},{32,40},... | collective-permute-start | bytes 2359304 | tf_op jit(solution)/shard_map/ppermute | solution.py:451
  57.4 2.5 %mixed_tail.1 = bf16[176,2048]{1,0:T(8,128)(2,1)} custom-call(bf16[384,2048]{1,0:T(8,128)(2,1)S(1)} %copy-done, bf16[384,2048]{1,0:T(8,128)(2,1)S(1)} %copy-done.1, bf16[384,2048]{1,0:T(8,128)(2,1)S(1)} %copy-done.2, bf16[3,7,2048]{2,1,0:T(8,128)(2,1)S(1)} %copy-done.5), custom_call_target="tpu_custom_call" | custom-call | flops 1000 | bytes 1000 | tf_op jit(solution)/shard_map/mixed_tail/pallas_call | solution.py:47
  59.9 0.0 copy-start.6
  59.9 0.0 collective-permute-done.14.refs_4_
  59.9 2.5 %collective-permute-start = (bf16[176,2048]{1,0:T(8,128)(2,1)}, bf16[176,2048]{1,0:T(8,128)(2,1)S(1)}, u32[]{:S(2)}, u32[]{:S(2)}) collective-permute-start(bf16[176,2048]{1,0:T(8,128)(2,1)} %mixed_tail.1), channel_id=1, source_target_pairs={{0,4},{4,8},{8,12},{12,16},{16,20},{20,24},{24,28},{28,32},{32,36}... | collective-permute-start | bytes 2162696 | tf_op jit(solution)/shard_map/ppermute | solution.py:492
  62.4 0.0 collective-permute-done.11.refs_1_
  62.4 0.0 collective-permute-done.12.refs_2_
  62.4 25.2 %attend.4 = (f32[2,144,1536]{2,1,0:T(8,128)S(1)}, f32[2,8,1536]{2,1,0:T(8,128)S(1)}, f32[1,144,1536]{2,1,0:T(8,128)S(1)}, f32[1,8,1536]{2,1,0:T(8,128)S(1)}) custom-call(s32[32,117]{1,0:T(8,128)S(1)} %copy-done.7, bf16[4,384,256]{2,1,0:T(8,128)(2,1)S(1)} %collective-permute-done.11.refs_1_, bf16[4,384,256]{2,1,0:T(8,128)(2,1)S(1)} %collective-permute-done.12.refs_2_, ...), custom_call_target="tpu_custom_call" | custom-call | flops 1000 | bytes 1000 | tf_op jit(solution)/shard_map/attend/pallas_call | solution.py:357
  87.6 0.0 collective-permute-done.10.refs_2_
  87.6 0.0 collective-permute-done.9.refs_1_
  87.6 0.0 copy-start.11
  87.7 0.0 copy-start.12
  87.7 17.3 %attend.5 = (bf16[384,1024]{1,0:T(8,128)(2,1)S(1)}, bf16[384,512]{1,0:T(8,128)(2,1)S(1)}) custom-call(s32[32,69]{1,0:T(8,128)S(1)} %copy-done.6, bf16[4,384,256]{2,1,0:T(8,128)(2,1)S(1)} %collective-permute-done.9.refs_1_, bf16[4,384,256]{2,1,0:T(8,128)(2,1)S(1)} %collective-permute-done.10.refs_2_, ...), custom_call_target="tpu_custom_call" | custom-call | flops 1000 | bytes 1000 | tf_op jit(solution)/shard_map/attend/pallas_call | solution.py:357
  104.9 1.3 collective-permute-start.15
  106.3 0.1 rev.3
  106.4 0.8 pad.4.rev
  107.1 0.0 collective-permute-done.halo
  107.1 0.9 copy-done.10
  108.0 12.2 %mixer.1 = (f32[384,2048]{1,0:T(8,128)}, f32[384,128]{1,0:T(8,128)}) custom-call(bf16[384,2048]{1,0:T(8,128)(2,1)} %one.3, bf16[384,2048]{1,0:T(8,128)(2,1)} %two.3, bf16[384,2048]{1,0:T(8,128)(2,1)} %val.3, bf16[176,2048]{1,0:T(8,128)(2,1)} %copy-done.10, bf16[3,7,2048]{2,1,0:T(8,128)(2,1)} %taps.3, f32[128,256]{1,0:T(8,128)} %pad.4.rev, bf16[384,2048]{1,0:T(8,128)(2,1)} %res.1), custom_call_target="tpu_custom_call" | custom-call | flops 1000 | bytes 1000 | tf_op jit(solution)/shard_map/mixer/pallas_call | solution.py:106
  120.1 1.1 reduce_sum.9
  121.2 0.0 collective-permute-done.15
  121.2 6.1 %collective-permute-start.16 = (f32[384]{0:T(512)S(1)}, f32[384]{0:T(512)S(1)}, u32[]{:S(2)}, u32[]{:S(2)}) collective-permute-start(f32[384]{0:T(512)S(1)} %reduce_sum.9), channel_id=1, source_target_pairs={{0,1},{1,0},{2,3},{3,2},{4,5},{5,4},{6,7},{7,6},{8,9},{9,8},{10,11... | collective-permute-start | bytes 4616 | tf_op jit(solution)/shard_map/ppermute | solution.py:505
  127.3 2.8 %collective-permute-start.17 = (f32[384]{0:T(512)S(1)}, f32[384]{0:T(512)S(1)}, u32[]{:S(2)}, u32[]{:S(2)}) collective-permute-start(f32[384]{0:T(512)S(1)} %reduce_sum.9), channel_id=1, source_target_pairs={{0,2},{1,3},{2,0},{3,1},{4,6},{5,7},{6,4},{7,5},{8,10},{9,11},{10,... | collective-permute-start | bytes 4616 | tf_op jit(solution)/shard_map/ppermute | solution.py:505
  130.1 0.5 collective-permute-start.18
  130.6 0.1 fusion
  130.6 1.0 pad_maximum_fusion.2
  131.6 0.0 collective-permute-done.16
  131.6 0.0 collective-permute-done.17
  131.6 3.0 %collective-permute-done.18 = f32[384]{0:T(512)S(1)} collective-permute-done((f32[384]{0:T(512)S(1)}, f32[384]{0:T(512)S(1)}, u32[]{:S(2)}, u32[]{:S(2)}) %collective-permute-start.18) | collective-permute-done | bytes 1568 | tf_op jit(solution)/shard_map/ppermute | solution.py:505
  134.6 1.5 %multiply_convert_fusion = bf16[384,2048]{1,0:T(8,128)(2,1)} fusion(f32[384,2048]{1,0:T(8,128)S(1)} %copy-done.9, f32[2048]{0:T(1024)S(1)} %convert_element_type.12, f32[384]{0:T(512)S(1)} %add_rsqrt_fusion), kind=kLoop, calls=%fused_computation | loop fusion | flops 2359296 | bytes 4728320 | tf_op jit(solution)/shard_map/convert_element_type | solution.py:509
  (20 shorter events, 0.0 us)
Async XLA Ops:
  0.6 26.4 %copy-start.3 = (bf16[384,1024]{1,0:T(8,128)(2,1)S(1)}, bf16[384,1024]{1,0:T(8,128)(2,1)}, u32[]{:S(2)}) copy-start(bf16[384,1024]{1,0:T(8,128)(2,1)} %queries.3) | copy-start | bytes 2359300
  2.7 21.6 %copy-start.13 = (bf16[384,512]{1,0:T(8,128)(2,1)S(1)}, bf16[384,512]{1,0:T(8,128)(2,1)}, u32[]{:S(2)}) copy-start(bf16[384,512]{1,0:T(8,128)(2,1)} %get-tuple-element.46) | copy-start | bytes 1179652
  2.7 6.0 %collective-permute-start.1 = (bf16[384,256]{1,0:T(8,128)(2,1)}, bf16[384,256]{1,0:T(8,128)(2,1)S(1)}, u32[]{:S(2)}, u32[]{:S(2)}) collective-permute-start(bf16[384,256]{1,0:T(8,128)(2,1)} %get-tuple-element.38), channel_id=1, source_target_pairs={{0,64},{4,68},{8,72},{12,76},{16,80},{20,84},{24,88},{28,92},{32,9... | collective-permute-start | bytes 589832 | tf_op jit(solution)/shard_map/ppermute | solution.py:451
  8.6 7.6 %collective-permute-start.2 = (bf16[384,256]{1,0:T(8,128)(2,1)}, bf16[384,256]{1,0:T(8,128)(2,1)S(1)}, u32[]{:S(2)}, u32[]{:S(2)}) collective-permute-start(bf16[384,256]{1,0:T(8,128)(2,1)} %get-tuple-element.38), channel_id=1, source_target_pairs={{0,16},{4,20},{8,24},{12,28},{16,32},{20,36},{24,40},{28,44},{32,4... | collective-permute-start | bytes 589832 | tf_op jit(solution)/shard_map/ppermute | solution.py:451
  10.3 6.2 %collective-permute-start.3 = (bf16[384,256]{1,0:T(8,128)(2,1)}, bf16[384,256]{1,0:T(8,128)(2,1)S(1)}, u32[]{:S(2)}, u32[]{:S(2)}) collective-permute-start(bf16[384,256]{1,0:T(8,128)(2,1)} %get-tuple-element.38), channel_id=1, source_target_pairs={{0,48},{4,52},{8,56},{12,60},{16,0},{20,4},{24,8},{28,12},{32,16},... | collective-permute-start | bytes 589832 | tf_op jit(solution)/shard_map/ppermute | solution.py:451
  12.4 9.0 %collective-permute-start.4 = (bf16[384,256]{1,0:T(8,128)(2,1)}, bf16[384,256]{1,0:T(8,128)(2,1)S(1)}, u32[]{:S(2)}, u32[]{:S(2)}) collective-permute-start(bf16[384,256]{1,0:T(8,128)(2,1)} %get-tuple-element.38), channel_id=1, source_target_pairs={{0,32},{4,36},{8,40},{12,44},{16,48},{20,52},{24,56},{28,60},{32,0... | collective-permute-start | bytes 589832 | tf_op jit(solution)/shard_map/ppermute | solution.py:451
  13.7 7.7 %collective-permute-start.5 = (bf16[384,256]{1,0:T(8,128)(2,1)S(1)}, bf16[384,256]{1,0:T(8,128)(2,1)S(1)}, u32[]{:S(2)}, u32[]{:S(2)}) collective-permute-start(bf16[384,256]{1,0:T(8,128)(2,1)S(1)} %collective-permute-done.1), channel_id=1, source_target_pairs={{0,4},{4,8},{8,12},{12,0},{16,20},{20,24},{24,28},{28,16},{32,36},... | collective-permute-start | bytes 589832 | tf_op jit(solution)/shard_map/ppermute | solution.py:451
  14.7 6.7 %collective-permute-start.6 = (bf16[384,256]{1,0:T(8,128)(2,1)S(1)}, bf16[384,256]{1,0:T(8,128)(2,1)S(1)}, u32[]{:S(2)}, u32[]{:S(2)}) collective-permute-start(bf16[384,256]{1,0:T(8,128)(2,1)S(1)} %collective-permute-done.1), channel_id=1, source_target_pairs={{0,12},{4,0},{8,4},{12,8},{16,28},{20,16},{24,20},{28,24},{32,44},... | collective-permute-start | bytes 589832 | tf_op jit(solution)/shard_map/ppermute | solution.py:451
  16.3 7.1 %collective-permute-start.7 = (bf16[384,256]{1,0:T(8,128)(2,1)S(1)}, bf16[384,256]{1,0:T(8,128)(2,1)S(1)}, u32[]{:S(2)}, u32[]{:S(2)}) collective-permute-start(bf16[384,256]{1,0:T(8,128)(2,1)S(1)} %collective-permute-done.1), channel_id=1, source_target_pairs={{0,8},{4,12},{8,0},{12,4},{16,24},{20,28},{24,16},{28,20},{32,40},... | collective-permute-start | bytes 589832 | tf_op jit(solution)/shard_map/ppermute | solution.py:451
  23.5 4.1 %copy-start.4 = (bf16[384,256]{1,0:T(8,128)(2,1)S(1)}, bf16[384,256]{1,0:T(8,128)(2,1)}, u32[]{:S(2)}) copy-start(bf16[384,256]{1,0:T(8,128)(2,1)} %get-tuple-element.38) | copy-start | bytes 589828
  23.5 31.8 %collective-permute-start.13 = (bf16[4,384,256]{2,1,0:T(8,128)(2,1)S(1)}, bf16[4,384,256]{2,1,0:T(8,128)(2,1)S(1)}, u32[]{:S(2)}, u32[]{:S(2)}) collective-permute-start(bf16[4,384,256]{2,1,0:T(8,128)(2,1)S(1)} %pad_maximum_fusion.1), channel_id=1, source_target_pairs={{0,16},{4,20},{8,24},{12,28},{16,32},{20,36},{24,40},{28,44},{32,4... | collective-permute-start | bytes 2359304 | tf_op jit(solution)/shard_map/ppermute | solution.py:451
  24.3 11.7 %collective-permute-start.8 = (bf16[384,512]{1,0:T(8,128)(2,1)S(1)}, bf16[384,512]{1,0:T(8,128)(2,1)S(1)}, u32[]{:S(2)}, u32[]{:S(2)}) collective-permute-start(bf16[384,512]{1,0:T(8,128)(2,1)S(1)} %copy-done.13), channel_id=1, source_target_pairs={{124,0},{120,4},{116,8},{112,12},{108,16},{104,20},{100,24},{96,28... | collective-permute-start | bytes 1179656 | tf_op jit(solution)/shard_map/ppermute | solution.py:484
  25.6 34.3 %collective-permute-start.14 = (bf16[4,384,256]{2,1,0:T(8,128)(2,1)S(1)}, bf16[4,384,256]{2,1,0:T(8,128)(2,1)S(1)}, u32[]{:S(2)}, u32[]{:S(2)}) collective-permute-start(bf16[4,384,256]{2,1,0:T(8,128)(2,1)S(1)} %pad_maximum_fusion.1), channel_id=1, source_target_pairs={{0,48},{4,52},{8,56},{12,60},{16,0},{20,4},{24,8},{28,12},{32,16},... | collective-permute-start | bytes 2359304 | tf_op jit(solution)/shard_map/ppermute | solution.py:451
  27.6 8.6 %copy-start.8 = (s32[32,69]{1,0:T(8,128)S(1)}, s32[32,69]{1,0:T(8,128)}, u32[]{:S(2)}) copy-start(s32[32,69]{1,0:T(8,128)} %constant.23.clone.refs_0_) | copy-start | bytes 26500
  27.7 34.7 %collective-permute-start.11 = (bf16[4,384,256]{2,1,0:T(8,128)(2,1)S(1)}, bf16[4,384,256]{2,1,0:T(8,128)(2,1)S(1)}, u32[]{:S(2)}, u32[]{:S(2)}) collective-permute-start(bf16[4,384,256]{2,1,0:T(8,128)(2,1)S(1)} %pad_maximum_fusion), channel_id=1, source_target_pairs={{0,4},{4,8},{8,12},{12,0},{16,20},{20,24},{24,28},{28,16},{32,36},... | collective-permute-start | bytes 2359304 | tf_op jit(solution)/shard_map/ppermute | solution.py:451
  29.8 32.6 %collective-permute-start.12 = (bf16[4,384,256]{2,1,0:T(8,128)(2,1)S(1)}, bf16[4,384,256]{2,1,0:T(8,128)(2,1)S(1)}, u32[]{:S(2)}, u32[]{:S(2)}) collective-permute-start(bf16[4,384,256]{2,1,0:T(8,128)(2,1)S(1)} %pad_maximum_fusion), channel_id=1, source_target_pairs={{0,12},{4,0},{8,4},{12,8},{16,28},{20,16},{24,20},{28,24},{32,44},... | collective-permute-start | bytes 2359304 | tf_op jit(solution)/shard_map/ppermute | solution.py:451
  36.0 21.4 %copy-start.2 = (bf16[384,2048]{1,0:T(8,128)(2,1)S(1)}, bf16[384,2048]{1,0:T(8,128)(2,1)}, u32[]{:S(2)}) copy-start(bf16[384,2048]{1,0:T(8,128)(2,1)} %val.3) | copy-start | bytes 4718596
  36.2 21.2 %copy-start = (bf16[384,2048]{1,0:T(8,128)(2,1)S(1)}, bf16[384,2048]{1,0:T(8,128)(2,1)}, u32[]{:S(2)}) copy-start(bf16[384,2048]{1,0:T(8,128)(2,1)} %one.3) | copy-start | bytes 4718596
  36.2 21.2 %copy-start.1 = (bf16[384,2048]{1,0:T(8,128)(2,1)S(1)}, bf16[384,2048]{1,0:T(8,128)(2,1)}, u32[]{:S(2)}) copy-start(bf16[384,2048]{1,0:T(8,128)(2,1)} %two.3) | copy-start | bytes 4718596
  36.2 21.1 %copy-start.5 = (bf16[3,7,2048]{2,1,0:T(8,128)(2,1)S(1)}, bf16[3,7,2048]{2,1,0:T(8,128)(2,1)}, u32[]{:S(2)}) copy-start(bf16[3,7,2048]{2,1,0:T(8,128)(2,1)} %taps.3) | copy-start | bytes 258052
  55.2 7.3 %copy-start.7 = (s32[32,117]{1,0:T(8,128)S(1)}, s32[32,117]{1,0:T(8,128)}, u32[]{:S(2)}) copy-start(s32[32,117]{1,0:T(8,128)} %constant.24.clone.refs_0_) | copy-start | bytes 44932
  55.2 32.4 %collective-permute-start.10 = (bf16[4,384,256]{2,1,0:T(8,128)(2,1)S(1)}, bf16[4,384,256]{2,1,0:T(8,128)(2,1)S(1)}, u32[]{:S(2)}, u32[]{:S(2)}) collective-permute-start(bf16[4,384,256]{2,1,0:T(8,128)(2,1)S(1)} %pad_maximum_fusion.1), channel_id=1, source_target_pairs={{0,32},{4,36},{8,40},{12,44},{16,48},{20,52},{24,56},{28,60},{32,0... | collective-permute-start | bytes 2359304 | tf_op jit(solution)/shard_map/ppermute | solution.py:451
  55.3 32.3 %collective-permute-start.9 = (bf16[4,384,256]{2,1,0:T(8,128)(2,1)S(1)}, bf16[4,384,256]{2,1,0:T(8,128)(2,1)S(1)}, u32[]{:S(2)}, u32[]{:S(2)}) collective-permute-start(bf16[4,384,256]{2,1,0:T(8,128)(2,1)S(1)} %pad_maximum_fusion), channel_id=1, source_target_pairs={{0,8},{4,12},{8,0},{12,4},{16,24},{20,28},{24,16},{28,20},{32,40},... | collective-permute-start | bytes 2359304 | tf_op jit(solution)/shard_map/ppermute | solution.py:451
  59.9 27.7 %copy-start.6 = (s32[32,69]{1,0:T(8,128)S(1)}, s32[32,69]{1,0:T(8,128)}, u32[]{:S(2)}) copy-start(s32[32,69]{1,0:T(8,128)} %constant.25.clone.refs_0_) | copy-start | bytes 26500
  59.9 47.2 %collective-permute-start = (bf16[176,2048]{1,0:T(8,128)(2,1)}, bf16[176,2048]{1,0:T(8,128)(2,1)S(1)}, u32[]{:S(2)}, u32[]{:S(2)}) collective-permute-start(bf16[176,2048]{1,0:T(8,128)(2,1)} %mixed_tail.1), channel_id=1, source_target_pairs={{0,4},{4,8},{8,12},{12,16},{16,20},{20,24},{24,28},{28,32},{32,36}... | collective-permute-start | bytes 2162696 | tf_op jit(solution)/shard_map/ppermute | solution.py:492
  87.6 18.6 %copy-start.11 = (bf16[128,128]{1,0:T(8,128)(2,1)S(1)}, bf16[128,128]{1,0:T(8,128)(2,1)}, u32[]{:S(2)}) copy-start(bf16[128,128]{1,0:T(8,128)(2,1)} %param.17) | copy-start | bytes 98308
  87.7 18.7 %copy-start.12 = (bf16[2048]{0:T(1024)(128)(2,1)S(1)}, bf16[2048]{0:T(1024)(128)(2,1)}, u32[]{:S(2)}) copy-start(bf16[2048]{0:T(1024)(128)(2,1)} %param.19) | copy-start | bytes 12292
  104.9 16.3 %collective-permute-start.15 = (bf16[384,512]{1,0:T(8,128)(2,1)S(1)}, bf16[384,512]{1,0:T(8,128)(2,1)S(1)}, u32[]{:S(2)}, u32[]{:S(2)}) collective-permute-start(bf16[384,512]{1,0:T(8,128)(2,1)S(1)} %get-tuple-element.61), channel_id=1, source_target_pairs={{0,124},{4,120},{8,116},{12,112},{16,108},{20,104},{24,100},{28,96... | collective-permute-start | bytes 1179656 | tf_op jit(solution)/shard_map/ppermute | solution.py:500
  107.1 0.9 copy-start.10
  121.2 10.4 %collective-permute-start.16 = (f32[384]{0:T(512)S(1)}, f32[384]{0:T(512)S(1)}, u32[]{:S(2)}, u32[]{:S(2)}) collective-permute-start(f32[384]{0:T(512)S(1)} %reduce_sum.9), channel_id=1, source_target_pairs={{0,1},{1,0},{2,3},{3,2},{4,5},{5,4},{6,7},{7,6},{8,9},{9,8},{10,11... | collective-permute-start | bytes 4616 | tf_op jit(solution)/shard_map/ppermute | solution.py:505
  127.3 4.3 %collective-permute-start.17 = (f32[384]{0:T(512)S(1)}, f32[384]{0:T(512)S(1)}, u32[]{:S(2)}, u32[]{:S(2)}) collective-permute-start(f32[384]{0:T(512)S(1)} %reduce_sum.9), channel_id=1, source_target_pairs={{0,2},{1,3},{2,0},{3,1},{4,6},{5,7},{6,4},{7,5},{8,10},{9,11},{10,... | collective-permute-start | bytes 4616 | tf_op jit(solution)/shard_map/ppermute | solution.py:505
  130.1 4.5 %collective-permute-start.18 = (f32[384]{0:T(512)S(1)}, f32[384]{0:T(512)S(1)}, u32[]{:S(2)}, u32[]{:S(2)}) collective-permute-start(f32[384]{0:T(512)S(1)} %reduce_sum.9), channel_id=1, source_target_pairs={{0,3},{1,2},{2,1},{3,0},{4,7},{5,6},{6,5},{7,4},{8,11},{9,10},{10,... | collective-permute-start | bytes 4616 | tf_op jit(solution)/shard_map/ppermute | solution.py:505
  130.6 4.1 %copy-start.9 = (f32[384,2048]{1,0:T(8,128)S(1)}, f32[384,2048]{1,0:T(8,128)}, u32[]{:S(2)}) copy-start(f32[384,2048]{1,0:T(8,128)} %get-tuple-element.63) | copy-start | bytes 9437188

commit v2 on v1

--- a/solution.py
+++ b/solution.py
@@ -53,7 +53,7 @@
         name="mixed_tail")(one, two, val, taps)
 
 
-def mixer_kernel(one, two, val, halo, taps, rev, res, branch, squares, x_scr, m_scr, t_scr):
+def mixer_kernel(one, two, val, halo, taps, rev, res, branch, sums, squares, x_scr, m_scr, t_scr):
     rows = one.shape[0]
     groups = LANES // GROUP
     span = BLK + TAPS
@@ -96,6 +96,10 @@
                     square += squares[r]
                 squares[r] = square
 
+    @pl.when(pl.program_id(0) == pl.num_programs(0) - 1)
+    def _():
+        sums[...] = jnp.sum(squares[...].T, axis=0, keepdims=True)
+
 
 def mixer_call(one, two, val, halo, taps, rev, res):
     rows, width = one.shape
@@ -107,9 +111,9 @@
         in_specs=[spec] * 3 + [pl.BlockSpec((halo.shape[0], tile), lambda i: (0, i)),
             pl.BlockSpec((3, SHORT, tile), lambda i: (0, 0, i)),
             pl.BlockSpec((groups, 2 * TAPS), lambda i: (i, 0)), spec],
-        out_specs=[spec, pl.BlockSpec((rows, LANES), lambda i: (0, 0))],
-        out_shape=[jax.ShapeDtypeStruct((rows, width), f32), jax.ShapeDtypeStruct((rows, LANES), f32)],
-        scratch_shapes=[pltpu.VMEM((units, 3, EDGE + rows, LANES), f32), pltpu.VMEM((units, TAPS + rows, LANES), bf),
+        out_specs=[spec, pl.BlockSpec((1, rows), lambda i: (0, 0))],
+        out_shape=[jax.ShapeDtypeStruct((rows, width), f32), jax.ShapeDtypeStruct((1, rows), f32)],
+        scratch_shapes=[pltpu.VMEM((rows, LANES), f32), pltpu.VMEM((units, 3, EDGE + rows, LANES), f32), pltpu.VMEM((units, TAPS + rows, LANES), bf),
             pltpu.VMEM((units, LANES // GROUP * BLK, 2 * TAPS), bf)],
         compiler_params=PARAMS,
         cost_estimate=LIGHT,
@@ -122,7 +126,10 @@
 
 
 HD = 128
-QUAD = 4
+UNIT = 2
+OWN, LENT = 4, 2
+UNITS = OWN + LENT
+UNROLL = 4
 ONES = 16
 EMPTY, FULL, DIAGONAL = 0, 1, 2
 DUMMIES = 3
@@ -150,7 +157,7 @@
 
 def turn_kernel(queries, turned):
     rows = queries.shape[0]
-    for head in range(QUAD):
+    for head in range(UNIT):
         wide = queries[:, head * HD:(head + 1) * HD].astype(f32).T * SCALE
         high = wide.astype(bf)
         columns = slice(head * rows, (head + 1) * rows)
@@ -160,11 +167,11 @@
 
 def turn_call(queries):
     rows, width = queries.shape
-    quads = width // (QUAD * HD)
-    return pl.pallas_call(turn_kernel, grid=(quads,),
-        in_specs=[pl.BlockSpec((rows, QUAD * HD), lambda i: (0, i))],
-        out_specs=pl.BlockSpec((1, 2 * HD, QUAD * rows), lambda i: (i, 0, 0)),
-        out_shape=jax.ShapeDtypeStruct((quads, 2 * HD, QUAD * rows), bf),
+    units = width // (UNIT * HD)
+    return pl.pallas_call(turn_kernel, grid=(units,),
+        in_specs=[pl.BlockSpec((rows, UNIT * HD), lambda i: (0, i))],
+        out_specs=pl.BlockSpec((1, 2 * HD, UNIT * rows), lambda i: (i, 0, 0)),
+        out_shape=jax.ShapeDtypeStruct((units, 2 * HD, UNIT * rows), bf),
         compiler_params=pltpu.CompilerParams(vmem_limit_bytes=ATTEND_VMEM), cost_estimate=LIGHT,
         name="turn_queries")(queries)
 
@@ -175,8 +182,8 @@
     at_b = at_a + shards
     at_live = at_b + shards
     at_fast = at_live + slots
-    at_slow = at_fast + 3 * (slots // 2)
-    return slots, at_a, at_b, at_live, at_fast, at_slow, at_slow + 3 * (slots // 2)
+    at_slow = at_fast + UNITS * (slots // 2)
+    return slots, at_a, at_b, at_live, at_fast, at_slow, at_slow + UNITS * (slots // 2)
 
 
 def attend_kernel(sizes, groups, starts, last, rows, *refs):
@@ -221,9 +228,9 @@
     at = 0
     for n, count in enumerate(groups):
         if starts[n]:
-            for quad in range(at, at + count):
-                acc[quad] = jnp.zeros(acc.shape[1:], f32)
-                top[quad] = jnp.full(top.shape[1:], -1e30, f32)
+            for unit in range(at, at + count):
+                acc[unit] = jnp.zeros(acc.shape[1:], f32)
+                top[unit] = jnp.full(top.shape[1:], -1e30, f32)
         at += count
     for slot, copy in copies:
         pl.when(slot >= 0)(copy.wait)
@@ -237,86 +244,82 @@
             kv[slot, :, HD:] = jnp.zeros((rows, HD), bf)
 
     def decode(code):
-        return code % 4, (code // 4) % 64, (code // 256) % 4, (code // 1024) % 4
-
-    def columns(pair):
-        return slice(pair * half, (pair + 1) * half)
-
-    def multiply_keys(quad, block, pair):
+        return code % 8, (code // 8) % 64, (code // 512) % 4, (code // 2048) % 4
+
+    def multiply_keys(unit, block):
         k = jnp.concatenate([kv[2 * block, :, :HD], kv[2 * block + 1, :, :HD]], axis=0)
         k = jnp.concatenate([k, k], axis=1)
-        return jnp.dot(k, q[quad, :, columns(pair)], preferred_element_type=f32)
-
-    def multiply_values(quad, block, pair, weights, factor):
+        return jnp.dot(k, q[unit], preferred_element_type=f32)
+
+    def multiply_values(unit, block, weights, factor):
         v = jnp.concatenate([kv[2 * block + n // parts, (n % parts) * HD:(n % parts + 1) * HD, HD:]
                              for n in range(2 * parts)], axis=1)
         live = [jnp.full((ONES, rows), table[me, at_live + 2 * block + n].astype(f32)).astype(bf) for n in range(2)]
         v = jnp.concatenate([v, jnp.concatenate(live, axis=1)], axis=0)
-        c = columns(pair)
-        acc[quad, :, c] = acc[quad, :, c] * factor + jnp.dot(v, weights, preferred_element_type=f32)
-
-    def soften(quad, pair, s):
-        c = columns(pair)
-        old = top[quad, 0:1, c]
+        acc[unit] = acc[unit] * factor + jnp.dot(v, weights, preferred_element_type=f32)
+
+    def soften(unit, s):
+        old = top[unit, 0:1]
         new = jnp.maximum(old, jnp.max(s, axis=0, keepdims=True))
-        top[quad, 0:1, c] = new
+        top[unit, 0:1] = new
         return jnp.exp2(s - new).astype(bf), jnp.exp2(old - new)
 
     @pl.loop(0, n_slow)
     def _(number):
-        quad, block, *modes = decode(table[me, at_slow + number])
+        unit, block, *modes = decode(table[me, at_slow + number])
         lead = (lax.broadcasted_iota(jnp.int32, (rows, rows), 0) - lax.broadcasted_iota(jnp.int32, (rows, rows), 1))
         lead = jnp.concatenate([lead, lead], axis=1)
         limits = [jnp.where(mode == FULL, rows, jnp.where(mode == DIAGONAL, 0, -2 * rows)) for mode in modes]
-        for pair in range(2):
-            s = multiply_keys(quad, block, pair)
-            s = jnp.concatenate([jnp.where(lead <= limits[n], s[n * rows:(n + 1) * rows], -1e30) for n in range(2)], axis=0)
-            weights, factor = soften(quad, pair, s)
-            multiply_values(quad, block, pair, weights, factor)
+        s = multiply_keys(unit, block)
+        s = jnp.concatenate([jnp.where(lead <= limits[n], s[n * rows:(n + 1) * rows], -1e30) for n in range(2)], axis=0)
+        weights, factor = soften(unit, s)
+        multiply_values(unit, block, weights, factor)
 
     def fast_entry(number):
         return decode(table[me, at_fast + jnp.clip(number, 0, n_fast - 1)])[:2]
 
     def region(number, unroll):
-        todo = [(*fast_entry(number + n), pair) for n in range(unroll) for pair in range(2)]
-        todo.append((*fast_entry(number + unroll), 0))
+        todo = [fast_entry(number + n) for n in range(unroll + 1)]
         s = s_scr[...]
-        pending = (*fast_entry(number - 1), 1, p_scr[...], a_scr[0:1])
-        for now, later in zip(todo, todo[1:]):
+        pending = (*fast_entry(number - 1), p_scr[...], a_scr[0:1])
+        for (unit, block), later in zip(todo, todo[1:]):
             coming = multiply_keys(*later)
             multiply_values(*pending)
-            quad, block, pair = now
-            weights, factor = soften(quad, pair, s)
-            pending = (quad, block, pair, weights, factor)
+            weights, factor = soften(unit, s)
+            pending = (unit, block, weights, factor)
             s = coming
         s_scr[...] = s
-        p_scr[...] = pending[3]
-        a_scr[0:1] = pending[4]
+        p_scr[...] = pending[2]
+        a_scr[0:1] = pending[3]
 
     @pl.when(n_fast > 0)
     def _():
-        s_scr[...] = multiply_keys(*fast_entry(0), 0)
+        s_scr[...] = multiply_keys(*fast_entry(0))
         p_scr[...] = jnp.zeros_like(p_scr)
         a_scr[...] = jnp.ones_like(a_scr)
 
-        @pl.loop(0, n_fast // 2)
+        @pl.loop(0, n_fast // UNROLL)
         def _(step):
-            region(2 * step, 2)
+            region(UNROLL * step, UNROLL)
+
+        @pl.when((n_fast // 2) % 2 == 1)
+        def _():
+            region(n_fast // UNROLL * UNROLL, 2)
 
         @pl.when(n_fast % 2 == 1)
         def _():
             region(n_fast - 1, 1)
 
-        multiply_values(*fast_entry(n_fast - 1), 1, p_scr[...], a_scr[0:1])
+        multiply_values(*fast_entry(n_fast - 1), p_scr[...], a_scr[0:1])
 
     if last:
         at = 0
         for n, count in enumerate(groups):
-            for quad in range(count):
-                for head in range(QUAD):
+            for unit in range(count):
+                for head in range(UNIT):
                     c = slice(head * rows, (head + 1) * rows)
-                    value = acc[at + quad, :HD, c] * (1.0 / acc[at + quad, HD:HD + 1, c])
-                    to = (quad * QUAD + head) * HD
+                    value = acc[at + unit, :HD, c] * (1.0 / acc[at + unit, HD:HD + 1, c])
+                    to = (unit * UNIT + head) * HD
                     results[n][:, to:to + HD] = value.T.astype(bf)
             at += count
     else:
@@ -335,18 +338,18 @@
 
 def attend_call(table, pieces, turned, states, last=False):
     wide = turned[0].shape[2]
-    rows = wide // QUAD
+    rows = wide // UNIT
     sizes = tuple(piece.shape[0] for piece in pieces)
     shards = sum(sizes)
     slots = table_layout(shards)[0]
     groups = tuple(t.shape[0] for t in turned)
-    quads = sum(groups)
+    units = sum(groups)
     starts = tuple(state is None for state in states)
     hbm = pl.BlockSpec(memory_space=pltpu.HBM)
     anywhere = pl.BlockSpec(memory_space=pl.ANY)
     operands = [table, *pieces, *turned] + [part for state in states if state is not None for part in state]
     if last:
-        out_shape = [jax.ShapeDtypeStruct((rows, count * QUAD * HD), bf) for count in groups]
+        out_shape = [jax.ShapeDtypeStruct((rows, count * UNIT * HD), bf) for count in groups]
         out_specs = [pl.BlockSpec(memory_space=pltpu.VMEM)] * len(groups)
     else:
         out_shape = []
@@ -360,10 +363,10 @@
         out_specs=out_specs,
         out_shape=out_shape,
         scratch_shapes=[
-            pltpu.VMEM((quads, 2 * HD, wide), bf),
+            pltpu.VMEM((units, 2 * HD, wide), bf),
             pltpu.VMEM((slots, rows, 2 * HD), bf),
-            pltpu.VMEM((quads, HD + ONES, wide), f32),
-            pltpu.VMEM((quads, 8, wide), f32),
+            pltpu.VMEM((units, HD + ONES, wide), f32),
+            pltpu.VMEM((units, 8, wide), f32),
             pltpu.VMEM((2 * rows, 2 * rows), f32),
             pltpu.VMEM((2 * rows, 2 * rows), bf),
             pltpu.VMEM((8, 2 * rows), f32),
@@ -382,7 +385,7 @@
 
 def make_table(sources_of, wants_of):
     lines = []
-    for me, sources in enumerate(sources_of):
+    for sources, wanted in zip(sources_of, wants_of):
         shards = len(sources)
         slots, at_a, at_b, at_live, at_fast, at_slow, size = table_layout(shards)
         line = np.zeros(size, np.int32)
@@ -408,19 +411,19 @@
 
         shared = []
         placed = set()
-        for quads, position, skipped in wants_of[me]:
+        for units, position, skipped in wanted:
             new = [(n, FULL if source < position else DIAGONAL) for n, source in enumerate(sources)
                    if source <= position and source not in skipped and n not in placed]
             new.sort(key=lambda member: member[1])
             blocks = place(new)
             placed.update(n for n, _ in new)
-            for quad in quads:
+            for unit in units:
                 for block, one, two in shared + blocks:
-                    code = quad + 4 * block
+                    code = unit + 8 * block
                     if (one, two) == (FULL, FULL):
                         fast.append(code)
                     else:
-                        slow.append(code + 256 * one + 1024 * two)
+                        slow.append(code + 512 * one + 2048 * two)
             shared = shared + [(block, FULL, FULL) for block, _, _ in blocks]
         assert used <= slots and len(dummies) <= DUMMIES
         line[0], line[1] = len(fast), len(slow)
@@ -435,7 +438,6 @@
 Z = Y = 4
 PLANE = Z * Y
 BLOCKS = 2 * PLANE
-SHARED = 9
 
 
 def neighbour(i, x=0, z=0, y=0):
@@ -462,17 +464,33 @@
     return [base] + line[1:], lines[0] + lines[1], lines[2]
 
 
-def wants(me):
-    found = [((0,) if mirrored(me) < SHARED else (0, 1), me, ())]
-    if me < SHARED:
-        found.append(((2,), mirrored(me), ()))
+def wants(me, lent):
+    found = [(tuple(range(OWN - lent.get(me, 0))), me, ())]
+    taken = lent.get(mirrored(me), 0)
+    if taken:
+        found.append((tuple(range(UNITS - taken, UNITS)), mirrored(me), ()))
     return found
 
 
+def source_lists():
+    everyone = range(BLOCKS)
+    return [[sources_of(me, 0, "z", "y")[n] + sources_of(me, 1, "y", "z")[n] for me in everyone] for n in range(3)]
+
+
 def tables():
-    everyone = range(BLOCKS)
-    stages = [[sources_of(me, 0, "z", "y")[n] + sources_of(me, 1, "y", "z")[n] for me in everyone] for n in range(3)]
-    return [make_table(stage, [wants(me) for me in everyone]) for stage in stages]
+    stages = source_lists()
+    lent = {}
+    for early in range(PLANE):
+        late = mirrored(early)
+        costs = []
+        for units in range(LENT + 1):
+            cost = []
+            for me in (early, late):
+                lines = [make_table([stage[me]], [wants(me, {late: units})]) for stage in stages]
+                cost.append(sum(int(line[0, 0]) + 1.3 * int(line[0, 1]) for line in lines))
+            costs.append((max(cost) + 0.01 * units, units))
+        lent[late] = min(costs)[1]
+    return [make_table(stage, [wants(me, lent) for me in range(BLOCKS)]) for stage in stages], lent
 
 
 def shards(stream_one, stream_two, stream_value, short_stream_taps, medium_filter, residual, norm_gain, queries, keys, values):
@@ -481,29 +499,30 @@
     me = lax.axis_index("ctx")
     own, given = pack_call(keys, values, queries)
     other = moved(own, x=1)
-    given = lax.ppermute(given, "ctx", [(mirrored(i), i) for i in range(SHARED)])
-    same, other = lax.optimization_barrier((own, other))
-    a = near_line(same, same, "z")
+    (near, far, across), lent = tables()
+    lenders = [i for i in range(BLOCKS) if lent.get(i, 0)]
+    given = lax.ppermute(given, "ctx", [(i, mirrored(i)) for i in lenders])
+    a = near_line(own, own, "z")
     b = near_line(other, other, "y")
-    a, b = lax.optimization_barrier((a, b))
+    a, b, given = lax.optimization_barrier((a, b, given))
     a_line, b_line = jnp.stack(a), jnp.stack(b)
     lines = [moved(a_line, y=1), moved(a_line, y=-1), moved(b_line, z=1), moved(b_line, z=-1)]
     tail = tail_call(stream_one, stream_two, stream_value, short_stream_taps)
     halo = lax.ppermute(tail, "ctx", [(i, i + 1) for i in range(BLOCKS - 1)])
-    near, far, across = tables()
     turned = [turn_call(queries), turn_call(given)]
     states = attend_call(near, [part[None] for part in a + b], turned, [None, None])
     a_line, b_line, states = lax.optimization_barrier((a_line, b_line, states))
     crossed = [moved(a_line, y=2), moved(b_line, z=2)]
     states = attend_call(far, lines, turned, states)
     kept, helped = attend_call(across, crossed, turned, states, last=True)
-    returned = lax.ppermute(helped, "ctx", [(i, mirrored(i)) for i in range(SHARED)])
+    returned = lax.ppermute(helped, "ctx", [(mirrored(i), i) for i in lenders])
     halo, helped = lax.optimization_barrier((halo, helped))
     branch, squares = mixer_call(stream_one, stream_two, stream_value, halo, short_stream_taps, reversed_taps(medium_filter), residual)
-    sums = jnp.sum(squares, axis=1)
+    sums = squares.reshape(rows)
     sums, returned = lax.optimization_barrier((sums, returned))
     parts = [lax.ppermute(sums, "tp", [(i, i ^ step) for i in range(4)]) for step in (1, 2, 3)]
-    later = jnp.where(me > BLOCKS - 1 - SHARED, returned, kept[:, middle:])
+    bound = jnp.array([OWN - lent.get(i, 0) for i in range(BLOCKS)], jnp.int32)[me] * (UNIT * HD) - middle
+    later = jnp.where(lax.broadcasted_iota(jnp.int32, returned.shape, 1) >= bound, returned, kept[:, middle:])
     attended = jnp.concatenate([kept[:, :middle], later], axis=1)
     scaling = lax.rsqrt((sums + parts[0] + parts[1] + parts[2]) / D + 1e-06)
     normed = (branch * scaling[:, None] * norm_gain.astype(f32)[None, :]).astype(bf)

time: 136 us -> 133 us (0.978)
  the two profiles are of different devices: /device:TPU:17 before, /device:TPU:97 now
where the time goes in v2:
time: 133 us
  Pallas kernels  68.3 us (51%)
  starting transfers between devices  37.2 us (28%)
  waiting for transfers between devices  19.6 us (15%)
  other arithmetic  3.46 us (3%)
  local copies, waits for them, and re-layouts  2.42 us (2%)
  between operations  1.66 us (1%)
    pallas_call x3, Pallas kernels, attend_call(): pl.pallas_call(functools.partial(attend_kernel, sizes, groups, starts, la...  50.4 us
    ppermute x13, waiting for transfers between devices, moved(): lax.ppermute(value, 'ctx', [(i, neighbour(i, x, z, y)) for i in range(BLO...  16.9 us
    ppermute x3, starting transfers between devices, shards(): lax.ppermute(sums, 'tp', [(i, i ^ step) for i in range(4)])  16.8 us
    ppermute x13, starting transfers between devices, moved(): lax.ppermute(value, 'ctx', [(i, neighbour(i, x, z, y)) for i in range(BLO...  15.4 us
    pallas_call x1, Pallas kernels, mixer_call(): pl.pallas_call(mixer_kernel, grid=(width // tile,), in_specs=[spec] * 3 +...  12.2 us
    ppermute x3, waiting for transfers between devices, shards(): lax.ppermute(sums, 'tp', [(i, i ^ step) for i in range(4)])  2.67 us
  transfers between devices with their start and end apart: 19, of which 5 were waited for; matrix products, arithmetic and copies ran while one was open for 3% of the time, Pallas kernels for 50%

profile of v2, /device:TPU:97, one launch (start us, length us, event | category | flops | bytes accessed | tf_op | source)
XLA Modules:
  0.0 132.6 jit_solution(15203496582813568201)
XLA Ops:
  0.6 2.0 %pack_keys.1 = (bf16[384,256]{1,0:T(8,128)(2,1)}, bf16[384,512]{1,0:T(8,128)(2,1)}) custom-call(bf16[384,128]{1,0:T(8,128)(2,1)} %keys.1, bf16[384,128]{1,0:T(8,128)(2,1)} %values.1, bf16[384,1024]{1,0:T(8,128)(2,1)} %queries.3), custom_call_target="tpu_custom_call" | custom-call | flops 1000 | bytes 1000 | tf_op jit(solution)/shard_map/pack_keys/pallas_call | solution.py:151
  2.7 1.2 collective-permute-start.4
  3.9 0.0 collective-permute-start.1
  3.9 1.5 %collective-permute-start.2 = (bf16[384,256]{1,0:T(8,128)(2,1)}, bf16[384,256]{1,0:T(8,128)(2,1)S(1)}, u32[]{:S(2)}, u32[]{:S(2)}) collective-permute-start(bf16[384,256]{1,0:T(8,128)(2,1)} %get-tuple-element.36), channel_id=1, source_target_pairs={{0,48},{4,52},{8,56},{12,60},{16,0},{20,4},{24,8},{28,12},{32,16},... | collective-permute-start | bytes 589832 | tf_op jit(solution)/shard_map/ppermute | solution.py:453
  5.3 1.3 collective-permute-start.8
  6.6 0.5 collective-permute-start.3
  7.2 1.5 %collective-permute-done.4 = bf16[384,256]{1,0:T(8,128)(2,1)S(1)} collective-permute-done((bf16[384,256]{1,0:T(8,128)(2,1)}, bf16[384,256]{1,0:T(8,128)(2,1)S(1)}, u32[]{:S(2)}, u32[]{:S(2)}) %collective-permute-start.4) | collective-permute-done | bytes 196640 | tf_op jit(solution)/shard_map/ppermute | solution.py:453
  8.6 1.3 collective-permute-start.5
  9.9 0.0 collective-permute-done.1
  9.9 2.3 %collective-permute-start.6 = (bf16[384,256]{1,0:T(8,128)(2,1)S(1)}, bf16[384,256]{1,0:T(8,128)(2,1)S(1)}, u32[]{:S(2)}, u32[]{:S(2)}) collective-permute-start(bf16[384,256]{1,0:T(8,128)(2,1)S(1)} %collective-permute-done.4), channel_id=1, source_target_pairs={{0,12},{4,0},{8,4},{12,8},{16,28},{20,16},{24,20},{28,24},{32,44},... | collective-permute-start | bytes 589832 | tf_op jit(solution)/shard_map/ppermute | solution.py:453
  12.3 1.5 %collective-permute-start.7 = (bf16[384,256]{1,0:T(8,128)(2,1)S(1)}, bf16[384,256]{1,0:T(8,128)(2,1)S(1)}, u32[]{:S(2)}, u32[]{:S(2)}) collective-permute-start(bf16[384,256]{1,0:T(8,128)(2,1)S(1)} %collective-permute-done.4), channel_id=1, source_target_pairs={{0,8},{4,12},{8,0},{12,4},{16,24},{20,28},{24,16},{28,20},{32,40},... | collective-permute-start | bytes 589832 | tf_op jit(solution)/shard_map/ppermute | solution.py:453
  13.8 0.3 collective-permute-done.3
  14.1 14.6 %collective-permute-done.5 = bf16[384,256]{1,0:T(8,128)(2,1)S(1)} collective-permute-done((bf16[384,256]{1,0:T(8,128)(2,1)S(1)}, bf16[384,256]{1,0:T(8,128)(2,1)S(1)}, u32[]{:S(2)}, u32[]{:S(2)}) %collective-permute-start.5) | collective-permute-done | bytes 196640 | tf_op jit(solution)/shard_map/ppermute | solution.py:453
  28.7 0.5 collective-permute-done.6
  29.3 0.0 collective-permute-done.7
  29.3 0.0 collective-permute-done.8.queries
  29.3 0.1 pad_maximum_fusion.1
  29.4 0.0 copy-start.4
  29.4 0.1 collective-permute-start.13
  29.5 1.5 %collective-permute-start.14 = (bf16[4,384,256]{2,1,0:T(8,128)(2,1)S(1)}, bf16[4,384,256]{2,1,0:T(8,128)(2,1)S(1)}, u32[]{:S(2)}, u32[]{:S(2)}) collective-permute-start(bf16[4,384,256]{2,1,0:T(8,128)(2,1)S(1)} %pad_maximum_fusion.1), channel_id=1, source_target_pairs={{0,48},{4,52},{8,56},{12,60},{16,0},{20,4},{24,8},{28,12},{32,16},... | collective-permute-start | bytes 2359304 | tf_op jit(solution)/shard_map/ppermute | solution.py:453
  30.9 0.8 turn_queries.2.refs_9_.refs_5_.refs_3_
  31.7 0.0 copy-start.8
  31.7 0.1 pad_maximum_fusion
  31.8 0.1 collective-permute-start.11
  32.0 3.4 %collective-permute-start.12 = (bf16[4,384,256]{2,1,0:T(8,128)(2,1)S(1)}, bf16[4,384,256]{2,1,0:T(8,128)(2,1)S(1)}, u32[]{:S(2)}, u32[]{:S(2)}) collective-permute-start(bf16[4,384,256]{2,1,0:T(8,128)(2,1)S(1)} %pad_maximum_fusion), channel_id=1, source_target_pairs={{0,12},{4,0},{8,4},{12,8},{16,28},{20,16},{24,20},{28,24},{32,44},... | collective-permute-start | bytes 2359304 | tf_op jit(solution)/shard_map/ppermute | solution.py:453
  35.4 0.4 turn_queries.3.refs_10_.refs_6_.refs_4_
  35.8 0.0 copy-start
  35.8 0.0 copy-start.1
  35.8 0.0 copy-start.5
  35.8 13.8 %attend.3 = (f32[4,144,768]{2,1,0:T(8,128)S(1)}, f32[4,8,768]{2,1,0:T(8,128)S(1)}, f32[2,144,768]{2,1,0:T(8,128)S(1)}, f32[2,8,768]{2,1,0:T(8,128)S(1)}) custom-call(s32[32,105]{1,0:T(8,128)S(1)} %copy-done.8, bf16[1,384,256]{2,1,0:T(8,128)(2,1)S(1)} %bitcast.10, bf16[1,384,256]{2,1,0:T(8,128)(2,1)S(1)} %bitcast.14, bf16[1,384,256]{2,1,0:T(8,128)(2,1)S(1)} %bitcast.16, ...), custom_call_target="tpu_custom_call" | custom-call | flops 1000 | bytes 1000 | tf_op jit(solution)/shard_map/attend/pallas_call | solution.py:360
  49.6 0.0 copy-start.6
  49.6 1.9 %collective-permute-start.10 = (bf16[4,384,256]{2,1,0:T(8,128)(2,1)S(1)}, bf16[4,384,256]{2,1,0:T(8,128)(2,1)S(1)}, u32[]{:S(2)}, u32[]{:S(2)}) collective-permute-start(bf16[4,384,256]{2,1,0:T(8,128)(2,1)S(1)} %pad_maximum_fusion.1), channel_id=1, source_target_pairs={{0,32},{4,36},{8,40},{12,44},{16,48},{20,52},{24,56},{28,60},{32,0... | collective-permute-start | bytes 2359304 | tf_op jit(solution)/shard_map/ppermute | solution.py:453
  51.6 0.0 collective-permute-done.13.refs_3_
  51.6 0.0 collective-permute-start.9
  51.6 2.5 %mixed_tail.1 = bf16[176,2048]{1,0:T(8,128)(2,1)} custom-call(bf16[384,2048]{1,0:T(8,128)(2,1)S(1)} %copy-done, bf16[384,2048]{1,0:T(8,128)(2,1)S(1)} %copy-done.1, bf16[384,2048]{1,0:T(8,128)(2,1)S(1)} %copy-done.2, bf16[3,7,2048]{2,1,0:T(8,128)(2,1)S(1)} %copy-done.5), custom_call_target="tpu_custom_call" | custom-call | flops 1000 | bytes 1000 | tf_op jit(solution)/shard_map/mixed_tail/pallas_call | solution.py:47
  54.1 0.0 copy-start.7
  54.1 0.0 collective-permute-done.14.refs_4_
  54.1 2.4 %collective-permute-start = (bf16[176,2048]{1,0:T(8,128)(2,1)}, bf16[176,2048]{1,0:T(8,128)(2,1)S(1)}, u32[]{:S(2)}, u32[]{:S(2)}) collective-permute-start(bf16[176,2048]{1,0:T(8,128)(2,1)} %mixed_tail.1), channel_id=1, source_target_pairs={{0,4},{4,8},{8,12},{12,16},{16,20},{20,24},{24,28},{28,32},{32,36}... | collective-permute-start | bytes 2162696 | tf_op jit(solution)/shard_map/ppermute | solution.py:511
  56.5 0.0 collective-permute-done.11.refs_1_
  56.5 22.4 %attend.4 = (f32[4,144,768]{2,1,0:T(8,128)S(1)}, f32[4,8,768]{2,1,0:T(8,128)S(1)}, f32[2,144,768]{2,1,0:T(8,128)S(1)}, f32[2,8,768]{2,1,0:T(8,128)S(1)}) custom-call(s32[32,177]{1,0:T(8,128)S(1)} %copy-done.6, bf16[4,384,256]{2,1,0:T(8,128)(2,1)S(1)} %collective-permute-done.11.refs_1_, bf16[4,384,256]{2,1,0:T(8,128)(2,1)S(1)} %collective-permute-done.12.refs_2_, ...), custom_call_target="tpu_custom_call" | custom-call | flops 1000 | bytes 1000 | tf_op jit(solution)/shard_map/attend/pallas_call | solution.py:360
  79.0 0.0 collective-permute-done.10.refs_2_
  79.0 0.0 collective-permute-done.9.refs_1_
  79.0 0.0 copy-start.11
  79.0 0.0 copy-start.12
  79.0 0.0 copy-start.13
  79.0 14.2 %attend.5 = (bf16[384,1024]{1,0:T(8,128)(2,1)S(1)}, bf16[384,512]{1,0:T(8,128)(2,1)S(1)}) custom-call(s32[32,105]{1,0:T(8,128)S(1)} %copy-done.7, bf16[4,384,256]{2,1,0:T(8,128)(2,1)S(1)} %collective-permute-done.9.refs_1_, bf16[4,384,256]{2,1,0:T(8,128)(2,1)S(1)} %collective-permute-done.10.refs_2_, ...), custom_call_target="tpu_custom_call" | custom-call | flops 1000 | bytes 1000 | tf_op jit(solution)/shard_map/attend/pallas_call | solution.py:360
  93.2 1.3 collective-permute-start.15
  94.5 0.1 rev.3
  94.6 0.8 pad.4.rev
  95.4 0.6 dynamic_slice.3
  96.7 0.0 collective-permute-done.halo
  96.8 0.0 copy-start.10
  96.8 0.8 copy-done.10
  97.6 12.2 %mixer.1 = (f32[384,2048]{1,0:T(8,128)}, f32[1,384]{1,0:T(1,128)}) custom-call(bf16[384,2048]{1,0:T(8,128)(2,1)} %one.3, bf16[384,2048]{1,0:T(8,128)(2,1)} %two.3, bf16[384,2048]{1,0:T(8,128)(2,1)} %val.3, bf16[176,2048]{1,0:T(8,128)(2,1)} %copy-done.10, bf16[3,7,2048]{2,1,0:T(8,128)(2,1)} %taps.3, f32[128,256]{1,0:T(8,128)} %pad.4.rev, bf16[384,2048]{1,0:T(8,128)(2,1)} %res.1), custom_call_target="tpu_custom_call" | custom-call | flops 1000 | bytes 1000 | tf_op jit(solution)/shard_map/mixer/pallas_call | solution.py:110
  109.8 0.7 reduce
  110.5 0.0 collective-permute-done.15
  110.6 13.6 %collective-permute-start.16 = (f32[384]{0:T(512)S(1)}, f32[384]{0:T(512)S(1)}, u32[]{:S(2)}, u32[]{:S(2)}) collective-permute-start(f32[384]{0:T(512)S(1)} %reduce), channel_id=1, source_target_pairs={{0,1},{1,0},{2,3},{3,2},{4,5},{5,4},{6,7},{7,6},{8,9},{9,8},{10,11... | collective-permute-start | bytes 4616 | tf_op jit(solution)/shard_map/ppermute | solution.py:523
  124.1 2.5 %collective-permute-start.17 = (f32[384]{0:T(512)S(1)}, f32[384]{0:T(512)S(1)}, u32[]{:S(2)}, u32[]{:S(2)}) collective-permute-start(f32[384]{0:T(512)S(1)} %reduce), channel_id=1, source_target_pairs={{0,2},{1,3},{2,0},{3,1},{4,6},{5,7},{6,4},{7,5},{8,10},{9,11},{10,... | collective-permute-start | bytes 4616 | tf_op jit(solution)/shard_map/ppermute | solution.py:523
  126.6 0.8 collective-permute-start.18
  127.4 0.1 fusion
  127.4 1.0 pad_maximum_fusion.2
  128.4 0.0 collective-permute-done.17
  128.4 2.7 %collective-permute-done.18 = f32[384]{0:T(512)S(1)} collective-permute-done((f32[384]{0:T(512)S(1)}, f32[384]{0:T(512)S(1)}, u32[]{:S(2)}, u32[]{:S(2)}) %collective-permute-start.18) | collective-permute-done | bytes 1568 | tf_op jit(solution)/shard_map/ppermute | solution.py:523
  131.1 1.5 %multiply_convert_fusion = bf16[384,2048]{1,0:T(8,128)(2,1)} fusion(f32[384,2048]{1,0:T(8,128)S(1)} %copy-done.9, f32[2048]{0:T(1024)S(1)} %convert_element_type.12, f32[384]{0:T(512)S(1)} %add_rsqrt_fusion), kind=kLoop, calls=%fused_computation | loop fusion | flops 2359296 | bytes 4728320 | tf_op jit(solution)/shard_map/convert_element_type | solution.py:528
  (22 shorter events, 0.1 us)
Async XLA Ops:
  0.6 30.3 %copy-start.3 = (bf16[384,1024]{1,0:T(8,128)(2,1)S(1)}, bf16[384,1024]{1,0:T(8,128)(2,1)}, u32[]{:S(2)}) copy-start(bf16[384,1024]{1,0:T(8,128)(2,1)} %queries.3) | copy-start | bytes 2359300
  2.7 6.0 %collective-permute-start.4 = (bf16[384,256]{1,0:T(8,128)(2,1)}, bf16[384,256]{1,0:T(8,128)(2,1)S(1)}, u32[]{:S(2)}, u32[]{:S(2)}) collective-permute-start(bf16[384,256]{1,0:T(8,128)(2,1)} %get-tuple-element.36), channel_id=1, source_target_pairs={{0,64},{4,68},{8,72},{12,76},{16,80},{20,84},{24,88},{28,92},{32,9... | collective-permute-start | bytes 589832 | tf_op jit(solution)/shard_map/ppermute | solution.py:453
  3.9 6.1 %collective-permute-start.1 = (bf16[384,256]{1,0:T(8,128)(2,1)}, bf16[384,256]{1,0:T(8,128)(2,1)S(1)}, u32[]{:S(2)}, u32[]{:S(2)}) collective-permute-start(bf16[384,256]{1,0:T(8,128)(2,1)} %get-tuple-element.36), channel_id=1, source_target_pairs={{0,16},{4,20},{8,24},{12,28},{16,32},{20,36},{24,40},{28,44},{32,4... | collective-permute-start | bytes 589832 | tf_op jit(solution)/shard_map/ppermute | solution.py:453
  3.9 8.4 %collective-permute-start.2 = (bf16[384,256]{1,0:T(8,128)(2,1)}, bf16[384,256]{1,0:T(8,128)(2,1)S(1)}, u32[]{:S(2)}, u32[]{:S(2)}) collective-permute-start(bf16[384,256]{1,0:T(8,128)(2,1)} %get-tuple-element.36), channel_id=1, source_target_pairs={{0,48},{4,52},{8,56},{12,60},{16,0},{20,4},{24,8},{28,12},{32,16},... | collective-permute-start | bytes 589832 | tf_op jit(solution)/shard_map/ppermute | solution.py:453
  5.3 23.9 %collective-permute-start.8 = (bf16[384,512]{1,0:T(8,128)(2,1)}, bf16[384,512]{1,0:T(8,128)(2,1)S(1)}, u32[]{:S(2)}, u32[]{:S(2)}) collective-permute-start(bf16[384,512]{1,0:T(8,128)(2,1)} %get-tuple-element.35), channel_id=1, source_target_pairs={{72,52},{76,48},{80,44},{84,40},{88,36},{92,32},{96,28},{100,24},{... | collective-permute-start | bytes 1179656 | tf_op jit(solution)/shard_map/ppermute | solution.py:504
  6.6 7.5 %collective-permute-start.3 = (bf16[384,256]{1,0:T(8,128)(2,1)}, bf16[384,256]{1,0:T(8,128)(2,1)S(1)}, u32[]{:S(2)}, u32[]{:S(2)}) collective-permute-start(bf16[384,256]{1,0:T(8,128)(2,1)} %get-tuple-element.36), channel_id=1, source_target_pairs={{0,32},{4,36},{8,40},{12,44},{16,48},{20,52},{24,56},{28,60},{32,0... | collective-permute-start | bytes 589832 | tf_op jit(solution)/shard_map/ppermute | solution.py:453
  8.6 20.1 %collective-permute-start.5 = (bf16[384,256]{1,0:T(8,128)(2,1)S(1)}, bf16[384,256]{1,0:T(8,128)(2,1)S(1)}, u32[]{:S(2)}, u32[]{:S(2)}) collective-permute-start(bf16[384,256]{1,0:T(8,128)(2,1)S(1)} %collective-permute-done.4), channel_id=1, source_target_pairs={{0,4},{4,8},{8,12},{12,0},{16,20},{20,24},{24,28},{28,16},{32,36},... | collective-permute-start | bytes 589832 | tf_op jit(solution)/shard_map/ppermute | solution.py:453
  9.9 19.3 %collective-permute-start.6 = (bf16[384,256]{1,0:T(8,128)(2,1)S(1)}, bf16[384,256]{1,0:T(8,128)(2,1)S(1)}, u32[]{:S(2)}, u32[]{:S(2)}) collective-permute-start(bf16[384,256]{1,0:T(8,128)(2,1)S(1)} %collective-permute-done.4), channel_id=1, source_target_pairs={{0,12},{4,0},{8,4},{12,8},{16,28},{20,16},{24,20},{28,24},{32,44},... | collective-permute-start | bytes 589832 | tf_op jit(solution)/shard_map/ppermute | solution.py:453
  12.3 17.0 %collective-permute-start.7 = (bf16[384,256]{1,0:T(8,128)(2,1)S(1)}, bf16[384,256]{1,0:T(8,128)(2,1)S(1)}, u32[]{:S(2)}, u32[]{:S(2)}) collective-permute-start(bf16[384,256]{1,0:T(8,128)(2,1)S(1)} %collective-permute-done.4), channel_id=1, source_target_pairs={{0,8},{4,12},{8,0},{12,4},{16,24},{20,28},{24,16},{28,20},{32,40},... | collective-permute-start | bytes 589832 | tf_op jit(solution)/shard_map/ppermute | solution.py:453
  29.4 2.4 %copy-start.4 = (bf16[384,256]{1,0:T(8,128)(2,1)S(1)}, bf16[384,256]{1,0:T(8,128)(2,1)}, u32[]{:S(2)}) copy-start(bf16[384,256]{1,0:T(8,128)(2,1)} %get-tuple-element.36) | copy-start | bytes 589828
  29.4 22.2 %collective-permute-start.13 = (bf16[4,384,256]{2,1,0:T(8,128)(2,1)S(1)}, bf16[4,384,256]{2,1,0:T(8,128)(2,1)S(1)}, u32[]{:S(2)}, u32[]{:S(2)}) collective-permute-start(bf16[4,384,256]{2,1,0:T(8,128)(2,1)S(1)} %pad_maximum_fusion.1), channel_id=1, source_target_pairs={{0,16},{4,20},{8,24},{12,28},{16,32},{20,36},{24,40},{28,44},{32,4... | collective-permute-start | bytes 2359304 | tf_op jit(solution)/shard_map/ppermute | solution.py:453
  29.5 24.7 %collective-permute-start.14 = (bf16[4,384,256]{2,1,0:T(8,128)(2,1)S(1)}, bf16[4,384,256]{2,1,0:T(8,128)(2,1)S(1)}, u32[]{:S(2)}, u32[]{:S(2)}) collective-permute-start(bf16[4,384,256]{2,1,0:T(8,128)(2,1)S(1)} %pad_maximum_fusion.1), channel_id=1, source_target_pairs={{0,48},{4,52},{8,56},{12,60},{16,0},{20,4},{24,8},{28,12},{32,16},... | collective-permute-start | bytes 2359304 | tf_op jit(solution)/shard_map/ppermute | solution.py:453
  31.7 4.1 %copy-start.8 = (s32[32,105]{1,0:T(8,128)S(1)}, s32[32,105]{1,0:T(8,128)}, u32[]{:S(2)}) copy-start(s32[32,105]{1,0:T(8,128)} %constant.32.clone.refs_0_) | copy-start | bytes 40324
  31.8 24.7 %collective-permute-start.11 = (bf16[4,384,256]{2,1,0:T(8,128)(2,1)S(1)}, bf16[4,384,256]{2,1,0:T(8,128)(2,1)S(1)}, u32[]{:S(2)}, u32[]{:S(2)}) collective-permute-start(bf16[4,384,256]{2,1,0:T(8,128)(2,1)S(1)} %pad_maximum_fusion), channel_id=1, source_target_pairs={{0,4},{4,8},{8,12},{12,0},{16,20},{20,24},{24,28},{28,16},{32,36},... | collective-permute-start | bytes 2359304 | tf_op jit(solution)/shard_map/ppermute | solution.py:453
  32.0 24.5 %collective-permute-start.12 = (bf16[4,384,256]{2,1,0:T(8,128)(2,1)S(1)}, bf16[4,384,256]{2,1,0:T(8,128)(2,1)S(1)}, u32[]{:S(2)}, u32[]{:S(2)}) collective-permute-start(bf16[4,384,256]{2,1,0:T(8,128)(2,1)S(1)} %pad_maximum_fusion), channel_id=1, source_target_pairs={{0,12},{4,0},{8,4},{12,8},{16,28},{20,16},{24,20},{28,24},{32,44},... | collective-permute-start | bytes 2359304 | tf_op jit(solution)/shard_map/ppermute | solution.py:453
  35.4 16.2 %copy-start.2 = (bf16[384,2048]{1,0:T(8,128)(2,1)S(1)}, bf16[384,2048]{1,0:T(8,128)(2,1)}, u32[]{:S(2)}) copy-start(bf16[384,2048]{1,0:T(8,128)(2,1)} %val.3) | copy-start | bytes 4718596
  35.8 15.8 %copy-start = (bf16[384,2048]{1,0:T(8,128)(2,1)S(1)}, bf16[384,2048]{1,0:T(8,128)(2,1)}, u32[]{:S(2)}) copy-start(bf16[384,2048]{1,0:T(8,128)(2,1)} %one.3) | copy-start | bytes 4718596
  35.8 15.8 %copy-start.1 = (bf16[384,2048]{1,0:T(8,128)(2,1)S(1)}, bf16[384,2048]{1,0:T(8,128)(2,1)}, u32[]{:S(2)}) copy-start(bf16[384,2048]{1,0:T(8,128)(2,1)} %two.3) | copy-start | bytes 4718596
  35.8 15.8 %copy-start.5 = (bf16[3,7,2048]{2,1,0:T(8,128)(2,1)S(1)}, bf16[3,7,2048]{2,1,0:T(8,128)(2,1)}, u32[]{:S(2)}) copy-start(bf16[3,7,2048]{2,1,0:T(8,128)(2,1)} %taps.3) | copy-start | bytes 258052
  49.6 6.9 %copy-start.6 = (s32[32,177]{1,0:T(8,128)S(1)}, s32[32,177]{1,0:T(8,128)}, u32[]{:S(2)}) copy-start(s32[32,177]{1,0:T(8,128)} %constant.33.clone.refs_0_) | copy-start | bytes 67972
  49.6 29.3 %collective-permute-start.10 = (bf16[4,384,256]{2,1,0:T(8,128)(2,1)S(1)}, bf16[4,384,256]{2,1,0:T(8,128)(2,1)S(1)}, u32[]{:S(2)}, u32[]{:S(2)}) collective-permute-start(bf16[4,384,256]{2,1,0:T(8,128)(2,1)S(1)} %pad_maximum_fusion.1), channel_id=1, source_target_pairs={{0,32},{4,36},{8,40},{12,44},{16,48},{20,52},{24,56},{28,60},{32,0... | collective-permute-start | bytes 2359304 | tf_op jit(solution)/shard_map/ppermute | solution.py:453
  51.6 27.4 %collective-permute-start.9 = (bf16[4,384,256]{2,1,0:T(8,128)(2,1)S(1)}, bf16[4,384,256]{2,1,0:T(8,128)(2,1)S(1)}, u32[]{:S(2)}, u32[]{:S(2)}) collective-permute-start(bf16[4,384,256]{2,1,0:T(8,128)(2,1)S(1)} %pad_maximum_fusion), channel_id=1, source_target_pairs={{0,8},{4,12},{8,0},{12,4},{16,24},{20,28},{24,16},{28,20},{32,40},... | collective-permute-start | bytes 2359304 | tf_op jit(solution)/shard_map/ppermute | solution.py:453
  54.1 24.9 %copy-start.7 = (s32[32,105]{1,0:T(8,128)S(1)}, s32[32,105]{1,0:T(8,128)}, u32[]{:S(2)}) copy-start(s32[32,105]{1,0:T(8,128)} %constant.34.clone.refs_0_) | copy-start | bytes 40324
  54.1 42.6 %collective-permute-start = (bf16[176,2048]{1,0:T(8,128)(2,1)}, bf16[176,2048]{1,0:T(8,128)(2,1)S(1)}, u32[]{:S(2)}, u32[]{:S(2)}) collective-permute-start(bf16[176,2048]{1,0:T(8,128)(2,1)} %mixed_tail.1), channel_id=1, source_target_pairs={{0,4},{4,8},{8,12},{12,16},{16,20},{20,24},{24,28},{28,32},{32,36}... | collective-permute-start | bytes 2162696 | tf_op jit(solution)/shard_map/ppermute | solution.py:511
  79.0 15.5 %copy-start.11 = (bf16[128,128]{1,0:T(8,128)(2,1)S(1)}, bf16[128,128]{1,0:T(8,128)(2,1)}, u32[]{:S(2)}) copy-start(bf16[128,128]{1,0:T(8,128)(2,1)} %param.18) | copy-start | bytes 98308
  79.0 15.6 %copy-start.12 = (bf16[2048]{0:T(1024)(128)(2,1)S(1)}, bf16[2048]{0:T(1024)(128)(2,1)}, u32[]{:S(2)}) copy-start(bf16[2048]{0:T(1024)(128)(2,1)} %param.20) | copy-start | bytes 12292
  79.0 16.4 %copy-start.13 = (s32[32]{0:T(128)S(1)}, s32[32]{0:T(128)}, u32[]{:S(2)}) copy-start(s32[32]{0:T(128)} %constant.35.clone) | copy-start | bytes 388
  93.2 17.3 %collective-permute-start.15 = (bf16[384,512]{1,0:T(8,128)(2,1)S(1)}, bf16[384,512]{1,0:T(8,128)(2,1)S(1)}, u32[]{:S(2)}, u32[]{:S(2)}) collective-permute-start(bf16[384,512]{1,0:T(8,128)(2,1)S(1)} %get-tuple-element.59), channel_id=1, source_target_pairs={{52,72},{48,76},{44,80},{40,84},{36,88},{32,92},{28,96},{24,100},{... | collective-permute-start | bytes 1179656 | tf_op jit(solution)/shard_map/ppermute | solution.py:518
  96.8 0.9 copy-start.10
  110.6 17.9 %collective-permute-start.16 = (f32[384]{0:T(512)S(1)}, f32[384]{0:T(512)S(1)}, u32[]{:S(2)}, u32[]{:S(2)}) collective-permute-start(f32[384]{0:T(512)S(1)} %reduce), channel_id=1, source_target_pairs={{0,1},{1,0},{2,3},{3,2},{4,5},{5,4},{6,7},{7,6},{8,9},{9,8},{10,11... | collective-permute-start | bytes 4616 | tf_op jit(solution)/shard_map/ppermute | solution.py:523
  124.1 4.3 %collective-permute-start.17 = (f32[384]{0:T(512)S(1)}, f32[384]{0:T(512)S(1)}, u32[]{:S(2)}, u32[]{:S(2)}) collective-permute-start(f32[384]{0:T(512)S(1)} %reduce), channel_id=1, source_target_pairs={{0,2},{1,3},{2,0},{3,1},{4,6},{5,7},{6,4},{7,5},{8,10},{9,11},{10,... | collective-permute-start | bytes 4616 | tf_op jit(solution)/shard_map/ppermute | solution.py:523
  126.6 4.5 %collective-permute-start.18 = (f32[384]{0:T(512)S(1)}, f32[384]{0:T(512)S(1)}, u32[]{:S(2)}, u32[]{:S(2)}) collective-permute-start(f32[384]{0:T(512)S(1)} %reduce), channel_id=1, source_target_pairs={{0,3},{1,2},{2,1},{3,0},{4,7},{5,6},{6,5},{7,4},{8,11},{9,10},{10,... | collective-permute-start | bytes 4616 | tf_op jit(solution)/shard_map/ppermute | solution.py:523
  127.4 3.7 %copy-start.9 = (f32[384,2048]{1,0:T(8,128)S(1)}, f32[384,2048]{1,0:T(8,128)}, u32[]{:S(2)}) copy-start(f32[384,2048]{1,0:T(8,128)} %get-tuple-element.61) | copy-start | bytes 9437188

commit v3 on v2

--- a/solution.py
+++ b/solution.py
@@ -490,6 +490,8 @@
                 cost.append(sum(int(line[0, 0]) + 1.3 * int(line[0, 1]) for line in lines))
             costs.append((max(cost) + 0.01 * units, units))
         lent[late] = min(costs)[1]
+    for late in range(PLANE + 1, BLOCKS):
+        lent[late] = max(lent[late], lent[late - 1])
     return [make_table(stage, [wants(me, lent) for me in range(BLOCKS)]) for stage in stages], lent
 
 
@@ -504,28 +506,33 @@
     given = lax.ppermute(given, "ctx", [(i, mirrored(i)) for i in lenders])
     a = near_line(own, own, "z")
     b = near_line(other, other, "y")
-    a, b, given = lax.optimization_barrier((a, b, given))
+    tail = tail_call(stream_one, stream_two, stream_value, short_stream_taps)
+    turned = turn_call(queries)
+    reverse = reversed_taps(medium_filter)
+    gain = norm_gain.astype(f32)[None, :]
+    a, b, given, tail, turned, reverse, gain = lax.optimization_barrier((a, b, given, tail, turned, reverse, gain))
     a_line, b_line = jnp.stack(a), jnp.stack(b)
     lines = [moved(a_line, y=1), moved(a_line, y=-1), moved(b_line, z=1), moved(b_line, z=-1)]
-    tail = tail_call(stream_one, stream_two, stream_value, short_stream_taps)
+    turned = [turned, turn_call(given)]
+    states = attend_call(near, [part[None] for part in a + b], turned, [None, None])
+    a_line, b_line, tail, states = lax.optimization_barrier((a_line, b_line, tail, states))
+    crossed = [moved(a_line, y=2), moved(b_line, z=2)]
     halo = lax.ppermute(tail, "ctx", [(i, i + 1) for i in range(BLOCKS - 1)])
-    turned = [turn_call(queries), turn_call(given)]
-    states = attend_call(near, [part[None] for part in a + b], turned, [None, None])
-    a_line, b_line, states = lax.optimization_barrier((a_line, b_line, states))
-    crossed = [moved(a_line, y=2), moved(b_line, z=2)]
     states = attend_call(far, lines, turned, states)
     kept, helped = attend_call(across, crossed, turned, states, last=True)
     returned = lax.ppermute(helped, "ctx", [(mirrored(i), i) for i in lenders])
     halo, helped = lax.optimization_barrier((halo, helped))
-    branch, squares = mixer_call(stream_one, stream_two, stream_value, halo, short_stream_taps, reversed_taps(medium_filter), residual)
-    sums = squares.reshape(rows)
+    branch, squares = mixer_call(stream_one, stream_two, stream_value, halo, short_stream_taps, reverse, residual)
+    sums = squares
     sums, returned = lax.optimization_barrier((sums, returned))
     parts = [lax.ppermute(sums, "tp", [(i, i ^ step) for i in range(4)]) for step in (1, 2, 3)]
-    bound = jnp.array([OWN - lent.get(i, 0) for i in range(BLOCKS)], jnp.int32)[me] * (UNIT * HD) - middle
+    least = [min(i for i in lenders if lent[i] > level) for level in range(LENT)]
+    count = sum((me >= bound).astype(jnp.int32) for bound in least)
+    bound = (OWN - count) * (UNIT * HD) - middle
     later = jnp.where(lax.broadcasted_iota(jnp.int32, returned.shape, 1) >= bound, returned, kept[:, middle:])
     attended = jnp.concatenate([kept[:, :middle], later], axis=1)
     scaling = lax.rsqrt((sums + parts[0] + parts[1] + parts[2]) / D + 1e-06)
-    normed = (branch * scaling[:, None] * norm_gain.astype(f32)[None, :]).astype(bf)
+    normed = (branch * scaling.reshape(rows, 1) * gain).astype(bf)
     return normed, attended
 
 

time: 133 us -> 136 us (1.023)
  the two profiles are of different devices: /device:TPU:97 before, /device:TPU:25 now
where the time goes in v3:
time: 136 us; the launch traced here: 135 us
  Pallas kernels  76.9 us (57%)
  starting transfers between devices  38 us (28%)
  waiting for transfers between devices  8.48 us (6%)
  local copies, waits for them, and re-layouts  5.81 us (4%)
  other arithmetic  5 us (4%)
    pallas_call x3, Pallas kernels, attend_call(): pl.pallas_call(functools.partial(attend_kernel, sizes, groups, starts, la...  58.9 us
    ppermute x13, starting transfers between devices, moved(): lax.ppermute(value, 'ctx', [(i, neighbour(i, x, z, y)) for i in range(BLO...  17.9 us
    ppermute x3, starting transfers between devices, shards(): lax.ppermute(sums, 'tp', [(i, i ^ step) for i in range(4)])  15.6 us
    pallas_call x1, Pallas kernels, mixer_call(): pl.pallas_call(mixer_kernel, grid=(width // tile,), in_specs=[spec] * 3 +...  12.3 us
    unnamed x36, local copies, waits for them, and re-layouts  4.21 us
    ppermute x1, waiting for transfers between devices, shards(): given = lax.ppermute(given, 'ctx', [(i, mirrored(i)) for i in lenders])  4.02 us
  transfers between devices with their start and end apart: 19, of which 3 were waited for; matrix products, arithmetic and copies ran while one was open for 3% of the time, Pallas kernels for 55%

profile of v3, /device:TPU:25, one launch (start us, length us, event | category | flops | bytes accessed | tf_op | source)
XLA Modules:
  0.0 135.2 jit_solution(11948208588583397597)
XLA Ops:
  0.6 0.0 copy-start
  0.6 2.1 %pack_keys.1 = (bf16[384,256]{1,0:T(8,128)(2,1)}, bf16[384,512]{1,0:T(8,128)(2,1)}) custom-call(bf16[384,128]{1,0:T(8,128)(2,1)} %keys.1, bf16[384,128]{1,0:T(8,128)(2,1)} %values.1, bf16[384,1024]{1,0:T(8,128)(2,1)} %queries.3), custom_call_target="tpu_custom_call" | custom-call | flops 1000 | bytes 1000 | tf_op jit(solution)/shard_map/pack_keys/pallas_call | solution.py:151
  2.7 1.2 collective-permute-start.3
  3.9 1.6 %collective-permute-start = (bf16[384,256]{1,0:T(8,128)(2,1)}, bf16[384,256]{1,0:T(8,128)(2,1)S(1)}, u32[]{:S(2)}, u32[]{:S(2)}) collective-permute-start(bf16[384,256]{1,0:T(8,128)(2,1)} %get-tuple-element.41), channel_id=1, source_target_pairs={{0,16},{4,20},{8,24},{12,28},{16,32},{20,36},{24,40},{28,44},{32,4... | collective-permute-start | bytes 589832 | tf_op jit(solution)/shard_map/ppermute | solution.py:453
  5.6 2.1 %collective-permute-start.1 = (bf16[384,256]{1,0:T(8,128)(2,1)}, bf16[384,256]{1,0:T(8,128)(2,1)S(1)}, u32[]{:S(2)}, u32[]{:S(2)}) collective-permute-start(bf16[384,256]{1,0:T(8,128)(2,1)} %get-tuple-element.41), channel_id=1, source_target_pairs={{0,48},{4,52},{8,56},{12,60},{16,0},{20,4},{24,8},{28,12},{32,16},... | collective-permute-start | bytes 589832 | tf_op jit(solution)/shard_map/ppermute | solution.py:453
  7.7 1.3 collective-permute-start.7
  9.0 1.4 %collective-permute-start.2 = (bf16[384,256]{1,0:T(8,128)(2,1)}, bf16[384,256]{1,0:T(8,128)(2,1)}, u32[]{:S(2)}, u32[]{:S(2)}) collective-permute-start(bf16[384,256]{1,0:T(8,128)(2,1)} %get-tuple-element.41), channel_id=1, source_target_pairs={{0,32},{4,36},{8,40},{12,44},{16,48},{20,52},{24,56},{28,60},{32,0... | collective-permute-start | bytes 589832 | tf_op jit(solution)/shard_map/ppermute | solution.py:453
  10.4 0.0 collective-permute-done.3
  10.4 0.0 collective-permute-start.4
  10.4 1.9 %collective-permute-done = bf16[384,256]{1,0:T(8,128)(2,1)S(1)} collective-permute-done((bf16[384,256]{1,0:T(8,128)(2,1)}, bf16[384,256]{1,0:T(8,128)(2,1)S(1)}, u32[]{:S(2)}, u32[]{:S(2)}) %collective-permute-start) | collective-permute-done | bytes 196640 | tf_op jit(solution)/shard_map/ppermute | solution.py:453
  12.2 0.5 collective-permute-start.5
  12.7 0.0 collective-permute-done.1
  12.7 0.7 copy-done.7
  13.4 0.7 collective-permute-start.6
  14.0 1.1 copy-done.3
  15.2 0.8 turn_queries.2.refs_9_.refs_5_.refs_3_
  16.0 0.1 copy-done.11
  16.1 1.4 %copy-done.2 = bf16[384,2048]{1,0:T(8,128)(2,1)S(1)} copy-done((bf16[384,2048]{1,0:T(8,128)(2,1)S(1)}, bf16[384,2048]{1,0:T(8,128)(2,1)}, u32[]{:S(2)}) %copy-start.2) | copy-done | bytes 1572888
  17.5 1.6 %mixed_tail.1 = bf16[176,2048]{1,0:T(8,128)(2,1)S(1)} custom-call(bf16[384,2048]{1,0:T(8,128)(2,1)S(1)} %copy-done, bf16[384,2048]{1,0:T(8,128)(2,1)S(1)} %copy-done.1, bf16[384,2048]{1,0:T(8,128)(2,1)S(1)} %copy-done.2, bf16[3,7,2048]{2,1,0:T(8,128)(2,1)S(1)} %copy-done.11), custom_call_target="tpu_custom_call" | custom-call | flops 1000 | bytes 1000 | tf_op jit(solution)/shard_map/mixed_tail/pallas_call | solution.py:47
  19.1 0.0 copy-start.9
  19.1 0.8 copy-done.9
  20.0 0.8 rev.3
  20.8 0.8 pad.4.rev
  21.6 0.0 collective-permute-done.2
  21.6 0.0 collective-permute-done.4
  21.6 0.0 collective-permute-done.5
  21.6 0.0 collective-permute-done.6
  21.6 4.0 %collective-permute-done.7.queries = bf16[384,512]{1,0:T(8,128)(2,1)} collective-permute-done((bf16[384,512]{1,0:T(8,128)(2,1)}, bf16[384,512]{1,0:T(8,128)(2,1)}, u32[]{:S(2)}, u32[]{:S(2)}) %collective-permute-start.7) | collective-permute-done | bytes 393248 | tf_op jit(solution)/shard_map/ppermute | solution.py:506
  25.7 1.2 pad_maximum_fusion
  26.9 0.0 copy-start.14
  26.9 4.1 %collective-permute-start.11 = (bf16[4,384,256]{2,1,0:T(8,128)(2,1)S(1)}, bf16[4,384,256]{2,1,0:T(8,128)(2,1)S(1)}, u32[]{:S(2)}, u32[]{:S(2)}) collective-permute-start(bf16[4,384,256]{2,1,0:T(8,128)(2,1)S(1)} %pad_maximum_fusion), channel_id=1, source_target_pairs={{0,4},{4,8},{8,12},{12,0},{16,20},{20,24},{24,28},{28,16},{32,36},... | collective-permute-start | bytes 2359304 | tf_op jit(solution)/shard_map/ppermute | solution.py:453
  31.0 0.0 collective-permute-start.12
  31.0 1.2 pad_maximum_fusion.1
  32.2 1.6 %collective-permute-start.13 = (bf16[4,384,256]{2,1,0:T(8,128)(2,1)S(1)}, bf16[4,384,256]{2,1,0:T(8,128)(2,1)S(1)}, u32[]{:S(2)}, u32[]{:S(2)}) collective-permute-start(bf16[4,384,256]{2,1,0:T(8,128)(2,1)S(1)} %pad_maximum_fusion.1), channel_id=1, source_target_pairs={{0,16},{4,20},{8,24},{12,28},{16,32},{20,36},{24,40},{28,44},{32,4... | collective-permute-start | bytes 2359304 | tf_op jit(solution)/shard_map/ppermute | solution.py:453
  33.8 4.2 %collective-permute-start.14 = (bf16[4,384,256]{2,1,0:T(8,128)(2,1)S(1)}, bf16[4,384,256]{2,1,0:T(8,128)(2,1)S(1)}, u32[]{:S(2)}, u32[]{:S(2)}) collective-permute-start(bf16[4,384,256]{2,1,0:T(8,128)(2,1)S(1)} %pad_maximum_fusion.1), channel_id=1, source_target_pairs={{0,48},{4,52},{8,56},{12,60},{16,0},{20,4},{24,8},{28,12},{32,16},... | collective-permute-start | bytes 2359304 | tf_op jit(solution)/shard_map/ppermute | solution.py:453
  38.0 1.3 turn_queries.3.refs_10_.refs_6_.refs_4_
  39.3 0.0 copy-start.10
  39.3 0.0 copy-start.12
  39.3 18.1 %attend.3 = (f32[4,144,768]{2,1,0:T(8,128)S(1)}, f32[4,8,768]{2,1,0:T(8,128)S(1)}, f32[2,144,768]{2,1,0:T(8,128)S(1)}, f32[2,8,768]{2,1,0:T(8,128)S(1)}) custom-call(s32[32,105]{1,0:T(8,128)S(1)} %copy-done.14, bf16[1,384,256]{2,1,0:T(8,128)(2,1)S(1)} %bitcast.11, bf16[1,384,256]{2,1,0:T(8,128)(2,1)S(1)} %bitcast.15, bf16[1,384,256]{2,1,0:T(8,128)(2,1)S(1)} %bitcast.17, ...), custom_call_target="tpu_custom_call" | custom-call | flops 1000 | bytes 1000 | tf_op jit(solution)/shard_map/attend/pallas_call | solution.py:360
  57.4 0.0 copy-start.13
  57.4 0.5 collective-permute-start.9
  58.0 0.0 collective-permute-done.11.refs_1_
  58.0 0.0 collective-permute-start.10
  58.0 0.0 collective-permute-done.12.refs_2_
  58.0 1.9 %collective-permute-start.8 = (bf16[176,2048]{1,0:T(8,128)(2,1)S(1)}, bf16[176,2048]{1,0:T(8,128)(2,1)}, u32[]{:S(2)}, u32[]{:S(2)}) collective-permute-start(bf16[176,2048]{1,0:T(8,128)(2,1)S(1)} %copy-done.10), channel_id=1, source_target_pairs={{0,4},{4,8},{8,12},{12,16},{16,20},{20,24},{24,28},{28,32},{32,36}... | collective-permute-start | bytes 2162696 | tf_op jit(solution)/shard_map/ppermute | solution.py:520
  59.9 0.0 collective-permute-done.13.refs_3_
  59.9 0.0 collective-permute-done.14.refs_4_
  59.9 23.2 %attend.4 = (f32[4,144,768]{2,1,0:T(8,128)S(1)}, f32[4,8,768]{2,1,0:T(8,128)S(1)}, f32[2,144,768]{2,1,0:T(8,128)S(1)}, f32[2,8,768]{2,1,0:T(8,128)S(1)}) custom-call(s32[32,177]{1,0:T(8,128)S(1)} %copy-done.12, bf16[4,384,256]{2,1,0:T(8,128)(2,1)S(1)} %collective-permute-done.11.refs_1_, bf16[4,384,256]{2,1,0:T(8,128)(2,1)S(1)} %collective-permute-done.12.refs_2_, ...), custom_call_target="tpu_custom_call" | custom-call | flops 1000 | bytes 1000 | tf_op jit(solution)/shard_map/attend/pallas_call | solution.py:360
  83.2 0.0 collective-permute-done.9.refs_1_
  83.2 0.0 collective-permute-done.10.refs_2_
  83.2 17.6 %attend.5 = (bf16[384,1024]{1,0:T(8,128)(2,1)S(1)}, bf16[384,512]{1,0:T(8,128)(2,1)S(1)}) custom-call(s32[32,105]{1,0:T(8,128)S(1)} %copy-done.13, bf16[4,384,256]{2,1,0:T(8,128)(2,1)S(1)} %collective-permute-done.9.refs_1_, bf16[4,384,256]{2,1,0:T(8,128)(2,1)S(1)} %collective-permute-done.10.refs_2_, ...), custom_call_target="tpu_custom_call" | custom-call | flops 1000 | bytes 1000 | tf_op jit(solution)/shard_map/attend/pallas_call | solution.py:360
  100.8 1.3 collective-permute-start.15
  102.1 0.0 collective-permute-done.8.halo
  102.2 12.3 %mixer.1 = (f32[384,2048]{1,0:T(8,128)}, f32[1,384]{1,0:T(1,128)}) custom-call(bf16[384,2048]{1,0:T(8,128)(2,1)} %one.3, bf16[384,2048]{1,0:T(8,128)(2,1)} %two.3, bf16[384,2048]{1,0:T(8,128)(2,1)} %val.3, bf16[176,2048]{1,0:T(8,128)(2,1)} %collective-permute-done.8.halo, bf16[3,7,2048]{2,1,0:T(8,128)(2,1)} %taps.3, f32[128,256]{1,0:T(8,128)} %pad.4.rev, ...), custom_call_target="tpu_custom_call" | custom-call | flops 1000 | bytes 1000 | tf_op jit(solution)/shard_map/mixer/pallas_call | solution.py:110
  114.4 0.0 collective-permute-done.15
  114.4 15.1 %collective-permute-start.18 = (f32[1,384]{1,0:T(1,128)}, f32[1,384]{1,0:T(1,128)S(1)}, u32[]{:S(2)}, u32[]{:S(2)}) collective-permute-start(f32[1,384]{1,0:T(1,128)} %get-tuple-element.72), channel_id=1, source_target_pairs={{0,3},{1,2},{2,1},{3,0},{4,7},{5,6},{6,5},{7,4},{8,11},{9,10},{10,... | collective-permute-start | bytes 4616 | tf_op jit(solution)/shard_map/ppermute | solution.py:528
  129.5 0.5 collective-permute-start.17
  130.0 0.0 collective-permute-start.16
  130.0 0.1 fusion
  130.1 1.0 pad_maximum_fusion.2
  131.1 0.0 collective-permute-done.18
  131.1 2.5 %collective-permute-done.17 = f32[1,384]{1,0:T(1,128)S(1)} collective-permute-done((f32[1,384]{1,0:T(1,128)}, f32[1,384]{1,0:T(1,128)S(1)}, u32[]{:S(2)}, u32[]{:S(2)}) %collective-permute-start.17) | collective-permute-done | bytes 1568 | tf_op jit(solution)/shard_map/ppermute | solution.py:528
  133.7 0.0 collective-permute-done.16
  133.7 1.5 %multiply_convert_fusion = bf16[384,2048]{1,0:T(8,128)(2,1)} fusion(f32[384,2048]{1,0:T(8,128)S(1)} %copy-done.15, f32[2048]{0:T(1024)S(1)} %broadcast_in_dim.7, f32[384]{0:T(512)S(1)} %rsqrt_reduce_fusion), kind=kLoop, calls=%fused_computation | loop fusion | flops 2359296 | bytes 4728320 | tf_op jit(solution)/shard_map/convert_element_type | solution.py:535
  (28 shorter events, 0.1 us)
Async XLA Ops:
  0.6 15.3 %copy-start = (bf16[384,2048]{1,0:T(8,128)(2,1)S(1)}, bf16[384,2048]{1,0:T(8,128)(2,1)}, u32[]{:S(2)}) copy-start(bf16[384,2048]{1,0:T(8,128)(2,1)} %one.3) | copy-start | bytes 4718596
  2.7 13.3 %copy-start.1 = (bf16[384,2048]{1,0:T(8,128)(2,1)S(1)}, bf16[384,2048]{1,0:T(8,128)(2,1)}, u32[]{:S(2)}) copy-start(bf16[384,2048]{1,0:T(8,128)(2,1)} %two.3) | copy-start | bytes 4718596
  2.7 7.6 %collective-permute-start.3 = (bf16[384,256]{1,0:T(8,128)(2,1)}, bf16[384,256]{1,0:T(8,128)(2,1)S(1)}, u32[]{:S(2)}, u32[]{:S(2)}) collective-permute-start(bf16[384,256]{1,0:T(8,128)(2,1)} %get-tuple-element.41), channel_id=1, source_target_pairs={{0,64},{4,68},{8,72},{12,76},{16,80},{20,84},{24,88},{28,92},{32,9... | collective-permute-start | bytes 589832 | tf_op jit(solution)/shard_map/ppermute | solution.py:453
  3.9 8.3 %collective-permute-start = (bf16[384,256]{1,0:T(8,128)(2,1)}, bf16[384,256]{1,0:T(8,128)(2,1)S(1)}, u32[]{:S(2)}, u32[]{:S(2)}) collective-permute-start(bf16[384,256]{1,0:T(8,128)(2,1)} %get-tuple-element.41), channel_id=1, source_target_pairs={{0,16},{4,20},{8,24},{12,28},{16,32},{20,36},{24,40},{28,44},{32,4... | collective-permute-start | bytes 589832 | tf_op jit(solution)/shard_map/ppermute | solution.py:453
  5.6 7.1 %collective-permute-start.1 = (bf16[384,256]{1,0:T(8,128)(2,1)}, bf16[384,256]{1,0:T(8,128)(2,1)S(1)}, u32[]{:S(2)}, u32[]{:S(2)}) collective-permute-start(bf16[384,256]{1,0:T(8,128)(2,1)} %get-tuple-element.41), channel_id=1, source_target_pairs={{0,48},{4,52},{8,56},{12,60},{16,0},{20,4},{24,8},{28,12},{32,16},... | collective-permute-start | bytes 589832 | tf_op jit(solution)/shard_map/ppermute | solution.py:453
  7.7 18.0 %collective-permute-start.7 = (bf16[384,512]{1,0:T(8,128)(2,1)}, bf16[384,512]{1,0:T(8,128)(2,1)}, u32[]{:S(2)}, u32[]{:S(2)}) collective-permute-start(bf16[384,512]{1,0:T(8,128)(2,1)} %get-tuple-element.40), channel_id=1, source_target_pairs={{72,52},{76,48},{80,44},{84,40},{88,36},{92,32},{96,28},{100,24},{... | collective-permute-start | bytes 1179656 | tf_op jit(solution)/shard_map/ppermute | solution.py:506
  9.0 12.6 %collective-permute-start.2 = (bf16[384,256]{1,0:T(8,128)(2,1)}, bf16[384,256]{1,0:T(8,128)(2,1)}, u32[]{:S(2)}, u32[]{:S(2)}) collective-permute-start(bf16[384,256]{1,0:T(8,128)(2,1)} %get-tuple-element.41), channel_id=1, source_target_pairs={{0,32},{4,36},{8,40},{12,44},{16,48},{20,52},{24,56},{28,60},{32,0... | collective-permute-start | bytes 589832 | tf_op jit(solution)/shard_map/ppermute | solution.py:453
  10.4 11.2 %collective-permute-start.4 = (bf16[384,256]{1,0:T(8,128)(2,1)S(1)}, bf16[384,256]{1,0:T(8,128)(2,1)}, u32[]{:S(2)}, u32[]{:S(2)}) collective-permute-start(bf16[384,256]{1,0:T(8,128)(2,1)S(1)} %collective-permute-done.3), channel_id=1, source_target_pairs={{0,4},{4,8},{8,12},{12,0},{16,20},{20,24},{24,28},{28,16},{32,36},... | collective-permute-start | bytes 589832 | tf_op jit(solution)/shard_map/ppermute | solution.py:453
  12.2 1.8 %copy-start.5 = (bf16[384,256]{1,0:T(8,128)(2,1)}, bf16[384,256]{1,0:T(8,128)(2,1)S(1)}, u32[]{:S(2)}) copy-start(bf16[384,256]{1,0:T(8,128)(2,1)S(1)} %collective-permute-done) | copy-start | bytes 589828
  12.2 9.4 %collective-permute-start.5 = (bf16[384,256]{1,0:T(8,128)(2,1)S(1)}, bf16[384,256]{1,0:T(8,128)(2,1)}, u32[]{:S(2)}, u32[]{:S(2)}) collective-permute-start(bf16[384,256]{1,0:T(8,128)(2,1)S(1)} %collective-permute-done.3), channel_id=1, source_target_pairs={{0,12},{4,0},{8,4},{12,8},{16,28},{20,16},{24,20},{28,24},{32,44},... | collective-permute-start | bytes 589832 | tf_op jit(solution)/shard_map/ppermute | solution.py:453
  12.7 0.7 copy-start.7
  13.4 8.2 %collective-permute-start.6 = (bf16[384,256]{1,0:T(8,128)(2,1)S(1)}, bf16[384,256]{1,0:T(8,128)(2,1)}, u32[]{:S(2)}, u32[]{:S(2)}) collective-permute-start(bf16[384,256]{1,0:T(8,128)(2,1)S(1)} %collective-permute-done.3), channel_id=1, source_target_pairs={{0,8},{4,12},{8,0},{12,4},{16,24},{20,28},{24,16},{28,20},{32,40},... | collective-permute-start | bytes 589832 | tf_op jit(solution)/shard_map/ppermute | solution.py:453
  14.0 1.1 copy-start.3
  15.2 0.9 copy-start.11
  16.1 1.4 %copy-start.2 = (bf16[384,2048]{1,0:T(8,128)(2,1)S(1)}, bf16[384,2048]{1,0:T(8,128)(2,1)}, u32[]{:S(2)}) copy-start(bf16[384,2048]{1,0:T(8,128)(2,1)} %val.3) | copy-start | bytes 4718596
  17.5 3.3 %copy-start.16 = (bf16[2048]{0:T(1024)(128)(2,1)S(1)}, bf16[2048]{0:T(1024)(128)(2,1)}, u32[]{:S(2)}) copy-start(bf16[2048]{0:T(1024)(128)(2,1)} %param.19) | copy-start | bytes 12292
  17.5 8.2 %copy-start.4 = (bf16[384,256]{1,0:T(8,128)(2,1)S(1)}, bf16[384,256]{1,0:T(8,128)(2,1)}, u32[]{:S(2)}) copy-start(bf16[384,256]{1,0:T(8,128)(2,1)} %get-tuple-element.41) | copy-start | bytes 589828
  19.1 0.9 copy-start.9
  26.9 12.4 %copy-start.6 = (bf16[384,256]{1,0:T(8,128)(2,1)S(1)}, bf16[384,256]{1,0:T(8,128)(2,1)}, u32[]{:S(2)}) copy-start(bf16[384,256]{1,0:T(8,128)(2,1)} %copy-done.5) | copy-start | bytes 589828
  26.9 12.4 %copy-start.8 = (bf16[384,256]{1,0:T(8,128)(2,1)S(1)}, bf16[384,256]{1,0:T(8,128)(2,1)}, u32[]{:S(2)}) copy-start(bf16[384,256]{1,0:T(8,128)(2,1)} %copy-done.7) | copy-start | bytes 589828
  26.9 12.4 %copy-start.14 = (s32[32,105]{1,0:T(8,128)S(1)}, s32[32,105]{1,0:T(8,128)}, u32[]{:S(2)}) copy-start(s32[32,105]{1,0:T(8,128)} %constant.31.clone.refs_0_) | copy-start | bytes 40324
  26.9 31.1 %collective-permute-start.11 = (bf16[4,384,256]{2,1,0:T(8,128)(2,1)S(1)}, bf16[4,384,256]{2,1,0:T(8,128)(2,1)S(1)}, u32[]{:S(2)}, u32[]{:S(2)}) collective-permute-start(bf16[4,384,256]{2,1,0:T(8,128)(2,1)S(1)} %pad_maximum_fusion), channel_id=1, source_target_pairs={{0,4},{4,8},{8,12},{12,0},{16,20},{20,24},{24,28},{28,16},{32,36},... | collective-permute-start | bytes 2359304 | tf_op jit(solution)/shard_map/ppermute | solution.py:453
  31.0 27.0 %collective-permute-start.12 = (bf16[4,384,256]{2,1,0:T(8,128)(2,1)S(1)}, bf16[4,384,256]{2,1,0:T(8,128)(2,1)S(1)}, u32[]{:S(2)}, u32[]{:S(2)}) collective-permute-start(bf16[4,384,256]{2,1,0:T(8,128)(2,1)S(1)} %pad_maximum_fusion), channel_id=1, source_target_pairs={{0,12},{4,0},{8,4},{12,8},{16,28},{20,16},{24,20},{28,24},{32,44},... | collective-permute-start | bytes 2359304 | tf_op jit(solution)/shard_map/ppermute | solution.py:453
  32.2 27.7 %collective-permute-start.13 = (bf16[4,384,256]{2,1,0:T(8,128)(2,1)S(1)}, bf16[4,384,256]{2,1,0:T(8,128)(2,1)S(1)}, u32[]{:S(2)}, u32[]{:S(2)}) collective-permute-start(bf16[4,384,256]{2,1,0:T(8,128)(2,1)S(1)} %pad_maximum_fusion.1), channel_id=1, source_target_pairs={{0,16},{4,20},{8,24},{12,28},{16,32},{20,36},{24,40},{28,44},{32,4... | collective-permute-start | bytes 2359304 | tf_op jit(solution)/shard_map/ppermute | solution.py:453
  33.8 26.1 %collective-permute-start.14 = (bf16[4,384,256]{2,1,0:T(8,128)(2,1)S(1)}, bf16[4,384,256]{2,1,0:T(8,128)(2,1)S(1)}, u32[]{:S(2)}, u32[]{:S(2)}) collective-permute-start(bf16[4,384,256]{2,1,0:T(8,128)(2,1)S(1)} %pad_maximum_fusion.1), channel_id=1, source_target_pairs={{0,48},{4,52},{8,56},{12,60},{16,0},{20,4},{24,8},{28,12},{32,16},... | collective-permute-start | bytes 2359304 | tf_op jit(solution)/shard_map/ppermute | solution.py:453
  39.3 18.7 %copy-start.10 = (bf16[176,2048]{1,0:T(8,128)(2,1)S(1)}, bf16[176,2048]{1,0:T(8,128)(2,1)}, u32[]{:S(2)}) copy-start(bf16[176,2048]{1,0:T(8,128)(2,1)} %copy-done.9) | copy-start | bytes 2162692
  39.3 20.6 %copy-start.12 = (s32[32,177]{1,0:T(8,128)S(1)}, s32[32,177]{1,0:T(8,128)}, u32[]{:S(2)}) copy-start(s32[32,177]{1,0:T(8,128)} %constant.32.clone.refs_0_) | copy-start | bytes 67972
  57.4 25.8 %copy-start.13 = (s32[32,105]{1,0:T(8,128)S(1)}, s32[32,105]{1,0:T(8,128)}, u32[]{:S(2)}) copy-start(s32[32,105]{1,0:T(8,128)} %constant.33.clone.refs_0_) | copy-start | bytes 40324
  57.4 25.8 %collective-permute-start.9 = (bf16[4,384,256]{2,1,0:T(8,128)(2,1)S(1)}, bf16[4,384,256]{2,1,0:T(8,128)(2,1)S(1)}, u32[]{:S(2)}, u32[]{:S(2)}) collective-permute-start(bf16[4,384,256]{2,1,0:T(8,128)(2,1)S(1)} %pad_maximum_fusion), channel_id=1, source_target_pairs={{0,8},{4,12},{8,0},{12,4},{16,24},{20,28},{24,16},{28,20},{32,40},... | collective-permute-start | bytes 2359304 | tf_op jit(solution)/shard_map/ppermute | solution.py:453
  58.0 25.2 %collective-permute-start.10 = (bf16[4,384,256]{2,1,0:T(8,128)(2,1)S(1)}, bf16[4,384,256]{2,1,0:T(8,128)(2,1)S(1)}, u32[]{:S(2)}, u32[]{:S(2)}) collective-permute-start(bf16[4,384,256]{2,1,0:T(8,128)(2,1)S(1)} %pad_maximum_fusion.1), channel_id=1, source_target_pairs={{0,32},{4,36},{8,40},{12,44},{16,48},{20,52},{24,56},{28,60},{32,0... | collective-permute-start | bytes 2359304 | tf_op jit(solution)/shard_map/ppermute | solution.py:453
  58.0 44.2 %collective-permute-start.8 = (bf16[176,2048]{1,0:T(8,128)(2,1)S(1)}, bf16[176,2048]{1,0:T(8,128)(2,1)}, u32[]{:S(2)}, u32[]{:S(2)}) collective-permute-start(bf16[176,2048]{1,0:T(8,128)(2,1)S(1)} %copy-done.10), channel_id=1, source_target_pairs={{0,4},{4,8},{8,12},{12,16},{16,20},{20,24},{24,28},{28,32},{32,36}... | collective-permute-start | bytes 2162696 | tf_op jit(solution)/shard_map/ppermute | solution.py:520
  100.8 13.6 %collective-permute-start.15 = (bf16[384,512]{1,0:T(8,128)(2,1)S(1)}, bf16[384,512]{1,0:T(8,128)(2,1)S(1)}, u32[]{:S(2)}, u32[]{:S(2)}) collective-permute-start(bf16[384,512]{1,0:T(8,128)(2,1)S(1)} %get-tuple-element.67), channel_id=1, source_target_pairs={{52,72},{48,76},{44,80},{40,84},{36,88},{32,92},{28,96},{24,100},{... | collective-permute-start | bytes 1179656 | tf_op jit(solution)/shard_map/ppermute | solution.py:523
  114.4 16.7 %collective-permute-start.18 = (f32[1,384]{1,0:T(1,128)}, f32[1,384]{1,0:T(1,128)S(1)}, u32[]{:S(2)}, u32[]{:S(2)}) collective-permute-start(f32[1,384]{1,0:T(1,128)} %get-tuple-element.72), channel_id=1, source_target_pairs={{0,3},{1,2},{2,1},{3,0},{4,7},{5,6},{6,5},{7,4},{8,11},{9,10},{10,... | collective-permute-start | bytes 4616 | tf_op jit(solution)/shard_map/ppermute | solution.py:528
  129.5 4.1 %collective-permute-start.17 = (f32[1,384]{1,0:T(1,128)}, f32[1,384]{1,0:T(1,128)S(1)}, u32[]{:S(2)}, u32[]{:S(2)}) collective-permute-start(f32[1,384]{1,0:T(1,128)} %get-tuple-element.72), channel_id=1, source_target_pairs={{0,2},{1,3},{2,0},{3,1},{4,6},{5,7},{6,4},{7,5},{8,10},{9,11},{10,... | collective-permute-start | bytes 4616 | tf_op jit(solution)/shard_map/ppermute | solution.py:528
  130.0 3.6 %collective-permute-start.16 = (f32[1,384]{1,0:T(1,128)}, f32[1,384]{1,0:T(1,128)S(1)}, u32[]{:S(2)}, u32[]{:S(2)}) collective-permute-start(f32[1,384]{1,0:T(1,128)} %get-tuple-element.72), channel_id=1, source_target_pairs={{0,1},{1,0},{2,3},{3,2},{4,5},{5,4},{6,7},{7,6},{8,9},{9,8},{10,11... | collective-permute-start | bytes 4616 | tf_op jit(solution)/shard_map/ppermute | solution.py:528
  130.0 3.6 %copy-start.17 = (f32[1,384]{1,0:T(1,128)S(1)}, f32[1,384]{1,0:T(1,128)}, u32[]{:S(2)}) copy-start(f32[1,384]{1,0:T(1,128)} %get-tuple-element.72) | copy-start | bytes 4612
  130.0 3.7 %copy-start.15 = (f32[384,2048]{1,0:T(8,128)S(1)}, f32[384,2048]{1,0:T(8,128)}, u32[]{:S(2)}) copy-start(f32[384,2048]{1,0:T(8,128)} %get-tuple-element.70) | copy-start | bytes 9437188
